TPU v7x, 1024 devices: a whole 8x8x8 slice. The times are simulated.
1024 devices in a mesh: rep: 4 (over y_hi), fsdp: 256 (over z, y_lo, x, core).
Axes of the slice: x: 8, y: 8 (y_hi: 4, y_lo: 2; y = y_hi * 2 + y_lo), z: 8, core: 2. Of those that a mesh axis runs over, the one named last changes fastest.
Arguments:
- acts: bfloat16 [4, 49152, 8192], P('rep', 'fsdp'), may hold values from -24 to 24
- targets: bfloat16 [4, 49152, 128], P('rep', 'fsdp'), may hold values from -6 to 6
- weight: float32 [4, 8192, 128], P('rep', 'fsdp'), may hold values from -5 to 5
- first_moment: float32 [4, 8192, 128], P('rep', 'fsdp'), may hold values from -0.001953125 to 0.001953125
- second_moment: float32 [4, 8192, 128], P('rep', 'fsdp'), may hold values from 3.7252903e-09 to 5.9604645e-08
- gain: float32 [4, 8192], P('rep', 'fsdp'), may hold values from 0.1 to 1.9
- gain_first: float32 [4, 8192], P('rep', 'fsdp'), may hold values from -0.25 to 0.25
- gain_second: float32 [4, 8192], P('rep', 'fsdp'), may hold values from 6.1035156e-05 to 0.0009765625
- base: float32 [8192, 128], P('fsdp'), may hold values from -5 to 5
- momentum: float32 [8192, 128], P('fsdp'), may hold values from -4 to 4
Outputs:
- new_weight: float32 [4, 8192, 128], P('rep', 'fsdp')
- new_gain: float32 [4, 8192], P('rep', 'fsdp')
- new_base: float32 [8192, 128], P('fsdp')
- new_momentum: float32 [8192, 128], P('fsdp')
All inputs are finite; a program needn't handle non-finite values.
Results may differ from a plain program's by a relative error of at most 0.0004.
Values may be sent and summed in bfloat16 or wider, within the bound.
A program may use at most 32 MiB of HBM per device.

v0:
```python
import math

import jax
import jax.numpy as jnp
from jax import lax
from jax.sharding import PartitionSpec as P

norm_eps = 1e-05
adam_eps = 1e-08
beta_first = 0.9
beta_second = 0.95
bias_first = 1.0 - 0.9**50
bias_second = 1.0 - 0.95**50
inner_rate = 0.1
decay_rate = 0.1
outer_rate = 0.7
nesterov = 0.9
mixing = 0.5


def normalize(block_rows):
    wide_rows = block_rows.astype(jnp.float32)
    factor = lax.rsqrt(jnp.mean(wide_rows * wide_rows, axis=-1, keepdims=True) + norm_eps)
    return (wide_rows * factor).astype(jnp.bfloat16)


def adam_step(param, grad, first, second):
    first = beta_first * first + (1.0 - beta_first) * grad
    second = beta_second * second + (1.0 - beta_second) * grad * grad
    update = first / bias_first / (jnp.sqrt(second / bias_second) + adam_eps)
    return param - inner_rate * (update + decay_rate * param)


def per_device(
    acts,
    targets,
    weight,
    first_moment,
    second_moment,
    gain,
    gain_first,
    gain_second,
    base,
    momentum,
):
    root_scale = 1.0 / math.sqrt(acts.shape[2])
    token_count = acts.shape[1] * lax.axis_size("fsdp")
    replica_count = lax.axis_size("rep")
    normed = normalize(acts[0])
    teacher = targets[0].astype(jnp.float32)
    own_weight = weight[0].astype(jnp.bfloat16)
    own_gain = gain[0].astype(jnp.bfloat16)
    full_weight, full_gain = (
        lax.all_gather(own_weight, "fsdp", axis=0, tiled=True),
        lax.all_gather(own_gain, "fsdp", axis=0, tiled=True),
    )
    hidden = (normed.astype(jnp.float32) * full_gain.astype(jnp.float32)).astype(jnp.bfloat16)
    key_rows = jnp.dot(hidden, full_weight, preferred_element_type=jnp.float32) * root_scale
    residual = (key_rows - teacher).astype(jnp.bfloat16)
    grad_full = lax.dot_general(
        normed, residual, (((0,), (0,)), ((), ())), preferred_element_type=jnp.float32
    )
    back_grad = (
        lax.dot_general(
            residual, full_weight, (((1,), (1,)), ((), ())), preferred_element_type=jnp.float32
        )
        * root_scale
    )
    gain_full = jnp.sum(normed.astype(jnp.float32) * back_grad, axis=0)
    grad_sum, gain_sum = (
        lax.psum_scatter(grad_full, "fsdp", scatter_dimension=0, tiled=True),
        lax.psum_scatter(gain_full, "fsdp", scatter_dimension=0, tiled=True),
    )
    grad_weight = own_gain.astype(jnp.float32)[:, None] * grad_sum * root_scale / token_count
    grad_gain = gain_sum / token_count
    inner_weight = adam_step(weight[0], grad_weight, first_moment[0], second_moment[0])
    new_gain = adam_step(gain[0], grad_gain, gain_first[0], gain_second[0])
    sent = base - inner_weight
    every_sent = lax.all_gather(sent[None], "rep", axis=0, tiled=True)
    average = jnp.sum(every_sent, axis=0) / replica_count
    new_momentum = nesterov * momentum + average
    new_base = base - outer_rate * (average + nesterov * new_momentum)
    new_weight = mixing * inner_weight + (1.0 - mixing) * new_base
    return (new_weight[None], new_gain[None], new_base, new_momentum)


def solution(mesh):
    return jax.shard_map(
        per_device,
        mesh=mesh,
        in_specs=(
            P("rep", "fsdp", None),
            P("rep", "fsdp", None),
            P("rep", "fsdp", None),
            P("rep", "fsdp", None),
            P("rep", "fsdp", None),
            P("rep", "fsdp"),
            P("rep", "fsdp"),
            P("rep", "fsdp"),
            P("fsdp", None),
            P("fsdp", None),
        ),
        out_specs=(P("rep", "fsdp", None), P("rep", "fsdp"), P("fsdp", None), P("fsdp", None)),
        check_vma=False,
    )
```

profile of v0, /device:TPU:32, one launch (start us, length us, event | category | flops | bytes accessed | tf_op | source)
XLA Modules:
  0.0 2276.2 jit_solution(7318137930574138304)
XLA Ops:
  7.2 0.0 all-gather.3.cloned.1.call-start
  7.2 1.3 bitcast_convert_fusion
  8.5 0.0 all-gather.3.cloned.1.call-update
  8.6 0.0 reduce-scatter.2.cloned.1.call-start
  8.6 1.4 fusion.38
  10.6 0.7 fusion.32
  11.3 0.2 dynamic-update-slice
  11.5 1114.0 %all-reduce = bf16[8192]{0:T(1024)(128)(2,1)S(1)} all-reduce(bf16[8192]{0:T(1024)(128)(2,1)S(1)} %dynamic-update-slice), channel_id=1, replica_groups=mesh['rep'=4,'fsdp'=256] {'fsdp'}, use_global_device_ids=true, to_apply=%add | all-reduce | flops 8192 | bytes 32768
  1125.5 2.6 fusion.2
  1128.1 0.0 all-gather.3.cloned.1.call-done
  1128.1 3.8 fusion.14
  1131.9 3.5 fusion.33
  1135.4 0.0 reduce-scatter.2.cloned.1.call-update
  1136.1 0.0 copy-start.6
  1136.1 0.0 copy-start.7
  1136.1 0.0 copy-start.2
  1136.1 0.0 copy-start.3
  1136.2 3.0 fusion.7
  1139.2 1095.7 %all-reduce.1 = f32[8192]{0:T(1024)S(1)} all-reduce(f32[8192]{0:T(1024)S(1)} %fusion.7), channel_id=4, replica_groups=mesh['rep'=4,'fsdp'=256] {'fsdp'}, use_global_device_ids=true, to_apply=%region_4.0.clone | all-reduce | flops 8192 | bytes 65536
  2234.9 0.6 fusion.31
  2235.5 18.7 reduce-scatter.2.cloned.1.call-done
  2254.2 0.8 fusion.36
  2255.0 13.7 all-gather
  2268.7 0.6 multiply_bitcast_fusion
  (18 shorter events, 0.1 us)
Async XLA Ops:
  7.2 1121.0 %all-gather.3.cloned.1.call-start = ((), (), s32[]{:S(2)}) async-start(), calls=%async_computation.1 | async-start | bytes 2105344 | tf_op jit(solution)/shard_map/all_gather | solution.py:54
  8.6 2245.7 %reduce-scatter.2.cloned.1.call-start = ((), (), s32[]{:S(2)}) async-start(), calls=%async_computation.2 | async-start | bytes 4210688 | tf_op jit(solution)/shard_map/reduce_scatter | solution.py:71
  1128.1 3.8 copy-start
  1136.1 1098.8 %copy-start.6 = (f32[1,32]{1,0:T(1,128)S(1)}, f32[1,32]{1,0:T(1,128)}, u32[]{:S(2)}) copy-start(f32[1,32]{1,0:T(1,128)} %param.15) | copy-start | bytes 388
  1136.1 1098.8 %copy-start.7 = (f32[1,32]{1,0:T(1,128)S(1)}, f32[1,32]{1,0:T(1,128)}, u32[]{:S(2)}) copy-start(f32[1,32]{1,0:T(1,128)} %param.17) | copy-start | bytes 388
  1136.1 1098.8 %copy-start.8 = (f32[1,32]{1,0:T(1,128)S(1)}, f32[1,32]{1,0:T(1,128)}, u32[]{:S(2)}) copy-start(f32[1,32]{1,0:T(1,128)} %param.16) | copy-start | bytes 388
  1136.1 1118.1 %copy-start.1 = (f32[32,128]{1,0:T(8,128)S(1)}, f32[32,128]{1,0:T(8,128)}, u32[]{:S(2)}) copy-start(f32[32,128]{1,0:T(8,128)} %param.18) | copy-start | bytes 49156
  1136.1 1118.1 %copy-start.2 = (f32[1,32,128]{2,1,0:T(8,128)S(1)}, f32[1,32,128]{2,1,0:T(8,128)}, u32[]{:S(2)}) copy-start(f32[1,32,128]{2,1,0:T(8,128)} %param.12) | copy-start | bytes 49156
  1136.1 1118.1 %copy-start.3 = (f32[1,32,128]{2,1,0:T(8,128)S(1)}, f32[1,32,128]{2,1,0:T(8,128)}, u32[]{:S(2)}) copy-start(f32[1,32,128]{2,1,0:T(8,128)} %param.14) | copy-start | bytes 49156
  1136.1 1118.1 %copy-start.4 = (f32[1,32,128]{2,1,0:T(8,128)S(1)}, f32[1,32,128]{2,1,0:T(8,128)}, u32[]{:S(2)}) copy-start(f32[1,32,128]{2,1,0:T(8,128)} %param.13) | copy-start | bytes 49156
  1136.1 1132.6 %copy-start.5 = (f32[32,128]{1,0:T(8,128)S(1)}, f32[32,128]{1,0:T(8,128)}, u32[]{:S(2)}) copy-start(f32[32,128]{1,0:T(8,128)} %param.19) | copy-start | bytes 49156
Sparse Core Ops, SparseCore 0:
  11.3 427.2 all-gather.2
  1135.5 1118.6 reduce-scatter.1
where the time goes:
time: 2280 us
  blocking collectives  2220 us (97%)
    unnamed x2, blocking collectives  2210 us
  transfers between devices with their start and end apart: 2, of which 1 were waited for; matrix products, arithmetic and copies ran while one was open for 0% of the time, Pallas kernels for 0%

commit v1 on v0

v1 whole, which is shorter than its diff:
```python
import functools
import math

import jax
import jax.numpy as jnp
from jax import lax
from jax.experimental import pallas as pl
from jax.experimental.pallas import tpu as pltpu
from jax.sharding import PartitionSpec as P

MESH = pl.DeviceIdType.MESH

norm_eps = 1e-05
adam_eps = 1e-08
beta_first = 0.9
beta_second = 0.95
bias_first = 1.0 - 0.9**50
bias_second = 1.0 - 0.95**50
inner_rate = 0.1
decay_rate = 0.1
outer_rate = 0.7
nesterov = 0.9
mixing = 0.5

SUBS = 4


def adam_step(param, grad, first, second):
    first = beta_first * first + (1.0 - beta_first) * grad
    second = beta_second * second + (1.0 - beta_second) * grad * grad
    update = first / bias_first / (jnp.sqrt(second / bias_second) + adam_eps)
    return param - inner_rate * (update + decay_rate * param)


def kernel(
    n,
    n_rep,
    acts_hbm,
    targets_hbm,
    weight_hbm,
    first_hbm,
    second_hbm,
    gain_hbm,
    gain_first_hbm,
    gain_second_hbm,
    base_hbm,
    momentum_hbm,
    new_weight_ref,
    new_gain_ref,
    new_base_ref,
    new_momentum_ref,
    acts,
    acts_t,
    targets,
    weight,
    first,
    second,
    gain,
    gain_first,
    gain_second,
    base,
    momentum,
    full_w,
    grads,
    from_core,
    out_plus,
    out_minus,
    in_plus,
    in_minus,
    mine,
    from_small,
    half_sum,
    from_y,
    drifts,
    sem_in,
    sem_small,
    sem_gp,
    sem_gm,
    sem_gc,
    sem_rc,
    sem_rp,
    sem_rm,
    sem_rs,
    sem_y,
    sem_rep,
):
    plus, minus = n // 2, n // 2 - 1
    tokens, d_model = acts.shape
    rows = weight.shape[0]
    token_count = tokens * 4 * n * n
    root_scale = 1.0 / math.sqrt(d_model)

    rep = lax.axis_index("rep")
    f = lax.axis_index("fsdp")
    c = lax.rem(f, 2)
    x = lax.rem(lax.div(f, 2), n)
    y = lax.rem(lax.div(f, 2 * n), 2)
    z = lax.div(f, 4 * n)
    s = x * (1 - c) + z * c
    b = z * (1 - c) + x * c

    def wrap(v):
        return lax.rem(v + n, n)

    def dev(ss, bb, yy):
        xx = ss * (1 - c) + bb * c
        zz = bb * (1 - c) + ss * c
        return ((zz * 2 + yy) * n + xx) * 2 + c

    sibling = f + 1 - 2 * c
    y_mate = dev(s, b, 1 - y)
    up, down = dev(s, wrap(b + 1), y), dev(s, wrap(b - 1), y)

    def remote(src, dst, sems, target):
        return pltpu.make_async_remote_copy(
            src_ref=src,
            dst_ref=dst,
            send_sem=sems[0],
            recv_sem=sems[1],
            device_id={"fsdp": target},
            device_id_type=MESH,
        )

    def pair(sem, *at):
        return sem.at[(0, *at)], sem.at[(1, *at)]

    loads = [
        pltpu.make_async_copy(src, dst, sem_in.at[i])
        for i, (src, dst) in enumerate(
            [
                (weight_hbm.at[0], weight),
                (gain_hbm, gain),
                (acts_hbm.at[0], acts),
                (targets_hbm.at[0], targets),
                (first_hbm.at[0], first),
                (second_hbm.at[0], second),
                (gain_first_hbm, gain_first),
                (gain_second_hbm, gain_second),
                (base_hbm, base),
                (momentum_hbm, momentum),
            ]
        )
    ]
    for load in loads:
        load.start()

    barrier = pltpu.get_barrier_semaphore()
    greeted = [sibling, y_mate, up, down]
    greeted += [dev(wrap(s + k), b, y) for k in range(1, n)]
    for target in greeted:
        pl.semaphore_signal(barrier, inc=1, device_id={"fsdp": target}, device_id_type=MESH)
    for k in range(1, n_rep):
        pl.semaphore_signal(
            barrier, inc=1, device_id={"rep": lax.rem(rep + k, n_rep)}, device_id_type=MESH
        )

    loads[0].wait()
    loads[1].wait()
    row_ids = lax.broadcasted_iota(jnp.int32, (rows, rows), 0)
    lane_ids = lax.broadcasted_iota(jnp.int32, (rows, rows), 1)
    eye = row_ids == lane_ids

    def to_column(row):
        return jnp.sum(jnp.where(eye, jnp.broadcast_to(row, (rows, rows)), 0.0), axis=1, keepdims=True)

    def to_row(column):
        return jnp.sum(jnp.where(eye, jnp.broadcast_to(column, (rows, rows)), 0.0), axis=0, keepdims=True)

    gain_used = to_column(gain[...].astype(jnp.bfloat16).astype(jnp.float32))
    low_weight = weight[...].astype(jnp.bfloat16).astype(jnp.float32)
    full_w[c, b, y, s] = (gain_used * low_weight).astype(jnp.bfloat16)
    pl.semaphore_wait(barrier, len(greeted) + n_rep - 1)

    gather_y = remote(full_w.at[c, b, y, s], full_w.at[c, b, y, s], pair(sem_y, 0), y_mate)
    gather_y.start()
    gather_y.wait_recv()
    gather_small = []
    for k in range(1, n):
        gather_small.append(
            remote(
                full_w.at[c, b, :, s],
                full_w.at[c, b, :, s],
                pair(sem_small, k - 1),
                dev(wrap(s + k), b, y),
            )
        )
        gather_small[-1].start()

    loads[2].wait()
    width = d_model // n

    def prepare(i, total):
        columns = pl.ds(pl.multiple_of(i * width, width), width)
        block = acts[:, columns]
        acts_t[columns, :] = block.T
        wide = block.astype(jnp.float32)
        square = wide * wide
        for j in range(width // 128):
            total = total + square[:, j * 128 : (j + 1) * 128]
        return total

    squares = lax.fori_loop(0, n, prepare, jnp.zeros((tokens, 128), jnp.float32))
    factor = lax.rsqrt(jnp.sum(squares, axis=1, keepdims=True) / d_model + norm_eps)

    for copy in gather_small:
        copy.wait_recv()

    half = n // 2

    def part(ref, j):
        return ref.at[j // 2, pl.ds((j % 2) * half, half)]

    def gather_plus(k, j):
        chunk = part(full_w.at[c, wrap(b - k)], j)
        return remote(chunk, chunk, pair(sem_gp, k, j), up)

    def gather_minus(k, j):
        chunk = part(full_w.at[c, wrap(b + k)], j)
        return remote(chunk, chunk, pair(sem_gm, k, j), down)

    def gather_core(i, owner, at):
        chunk = full_w.at[owner, wrap(at)]
        return remote(chunk, chunk, pair(sem_gc, i), sibling)

    core_offsets = [0] + [-1 - k for k in range(plus)] + [1 + k for k in range(minus)]
    for k in range(plus + 1):
        for j in range(SUBS):
            if k > 0:
                gather_plus(k - 1, j).wait_recv()
            if k < plus:
                gather_plus(k, j).start()
            if 0 < k <= minus:
                gather_minus(k - 1, j).wait_recv()
            if k < minus:
                gather_minus(k, j).start()
        if k == 0:
            gather_core(0, c, b).start()
        else:
            gather_core(k, c, b - k).start()
            if k <= minus:
                gather_core(plus + k, c, b + k).start()
    for i, offset in enumerate(core_offsets):
        gather_core(i, 1 - c, s + offset).wait_recv()

    def forward(i, total):
        columns = pl.ds(pl.multiple_of(i * width, width), width)
        pieces = []
        for yy in range(2):
            for xx in range(n):
                pieces.append(full_w[0, i, yy, xx])
                pieces.append(full_w[1, xx, yy, i])
        return total + jnp.dot(
            acts[:, columns], jnp.concatenate(pieces, axis=0), preferred_element_type=jnp.float32
        )

    keys = lax.fori_loop(0, n, forward, jnp.zeros((tokens, 128), jnp.float32))
    loads[3].wait()
    residual = keys * factor * root_scale - targets[...].astype(jnp.float32)
    scaled = (residual * factor).astype(jnp.bfloat16)

    def backward(i, carry):
        columns = pl.ds(pl.multiple_of(i * width, width), width)
        block = jnp.dot(acts_t[columns, :], scaled, preferred_element_type=jnp.float32)
        block = block.astype(jnp.bfloat16)
        at = 0
        for yy in range(2):
            for xx in range(n):
                grads[0, i, yy, xx] = block[at : at + rows]
                grads[1, xx, yy, i] = block[at + rows : at + 2 * rows]
                at += 2 * rows
        return carry

    lax.fori_loop(0, n, backward, 0)

    order = []
    for k in range(plus):
        order.append(plus - k)
        if k < minus:
            order.append(-(minus - k))
    order.append(0)

    def reduce_core(i, at, offset):
        chunk = wrap(at + offset)
        return remote(grads.at[1 - c, chunk], from_core.at[chunk], pair(sem_rc, i), sibling)

    for i, offset in enumerate(order):
        reduce_core(i, s, offset).start()

    def own(chunk, j):
        at = (j // 2, pl.ds((j % 2) * half, half))
        return grads[(c, chunk, *at)].astype(jnp.float32) + from_core[(chunk, *at)].astype(jnp.float32)

    def reduce_plus(k, j):
        return remote(part(out_plus.at[k], j), part(in_plus.at[k], j), pair(sem_rp, k, j), up)

    def reduce_minus(k, j):
        return remote(part(out_minus.at[k], j), part(in_minus.at[k], j), pair(sem_rm, k, j), down)

    def reduce_core_wait(offset):
        i = order.index(offset)
        chunk = wrap(b + offset)
        remote(grads.at[c, chunk], from_core.at[chunk], pair(sem_rc, i), sibling).wait_recv()

    for k in range(plus):
        reduce_core_wait(plus - k)
        if k < minus:
            reduce_core_wait(-(minus - k))
        for j in range(SUBS):
            at = (j // 2, pl.ds((j % 2) * half, half))
            value = own(wrap(b + plus - k), j)
            if k > 0:
                reduce_plus(k - 1, j).wait_recv()
                value = value + in_plus[(k - 1, *at)].astype(jnp.float32)
            out_plus[(k, *at)] = value.astype(jnp.bfloat16)
            reduce_plus(k, j).start()
            if k < minus:
                value = own(wrap(b - (minus - k)), j)
                if k > 0:
                    reduce_minus(k - 1, j).wait_recv()
                    value = value + in_minus[(k - 1, *at)].astype(jnp.float32)
                out_minus[(k, *at)] = value.astype(jnp.bfloat16)
                reduce_minus(k, j).start()
    reduce_core_wait(0)
    for j in range(SUBS):
        at = (j // 2, pl.ds((j % 2) * half, half))
        value = own(b, j)
        reduce_plus(plus - 1, j).wait_recv()
        value = value + in_plus[(plus - 1, *at)].astype(jnp.float32)
        if minus > 0:
            reduce_minus(minus - 1, j).wait_recv()
            value = value + in_minus[(minus - 1, *at)].astype(jnp.float32)
        mine[at] = value.astype(jnp.bfloat16)

    reduce_small = []
    for k in range(1, n):
        peer = wrap(s + k)
        reduce_small.append(
            remote(mine.at[:, peer], from_small.at[k - 1], pair(sem_rs, k - 1), dev(peer, b, y))
        )
        reduce_small[-1].start()
    for load in loads[4:]:
        load.wait()
    total = mine[:, s].astype(jnp.float32)
    for k in range(1, n):
        reduce_small[k - 1].wait_recv()
        total = total + from_small[k - 1].astype(jnp.float32)
    half_sum[...] = total
    reduce_y = remote(half_sum.at[1 - y], from_y, pair(sem_y, 1), y_mate)
    reduce_y.start()
    reduce_y.wait_recv()
    grad_sum = half_sum[y] + from_y[...]

    grad_weight = gain_used * grad_sum * root_scale / token_count
    inner_weight = adam_step(weight[...], grad_weight, first[...], second[...])
    drifts[rep] = base[...] - inner_weight
    rep_copies = []
    for k in range(1, n_rep):
        rep_copies.append(
            pltpu.make_async_remote_copy(
                src_ref=drifts.at[rep],
                dst_ref=drifts.at[rep],
                send_sem=sem_rep.at[0, k - 1],
                recv_sem=sem_rep.at[1, k - 1],
                device_id={"rep": lax.rem(rep + k, n_rep)},
                device_id_type=MESH,
            )
        )
        rep_copies[-1].start()

    gain_sum = to_row(jnp.sum(grad_sum * low_weight, axis=1, keepdims=True) * root_scale)
    new_gain_ref[...] = adam_step(gain[...], gain_sum / token_count, gain_first[...], gain_second[...])

    for copy in rep_copies:
        copy.wait_recv()
    average = drifts[0]
    for k in range(1, n_rep):
        average = average + drifts[k]
    average = average / n_rep
    new_momentum = nesterov * momentum[...] + average
    new_base = base[...] - outer_rate * (average + nesterov * new_momentum)
    new_momentum_ref[...] = new_momentum
    new_base_ref[...] = new_base
    new_weight_ref[0] = mixing * inner_weight + (1.0 - mixing) * new_base

    gather_y.wait_send()
    reduce_y.wait_send()
    for copy in gather_small + reduce_small + rep_copies:
        copy.wait_send()
    for k in range(plus):
        for j in range(SUBS):
            gather_plus(k, j).wait_send()
            reduce_plus(k, j).wait_send()
    for k in range(minus):
        for j in range(SUBS):
            gather_minus(k, j).wait_send()
            reduce_minus(k, j).wait_send()
    for i, offset in enumerate(core_offsets):
        gather_core(i, c, b + offset).wait_send()
    for i, offset in enumerate(order):
        reduce_core(i, s, offset).wait_send()


def per_device(*args):
    acts, targets, weight, _, _, gain = args[:6]
    n_rep = lax.axis_size("rep")
    n = math.isqrt(lax.axis_size("fsdp") // 4)
    plus, minus = n // 2, max(n // 2 - 1, 1)
    tokens, d_model = acts.shape[1:]
    rows, head = weight.shape[1:]
    low, wide = jnp.bfloat16, jnp.float32
    chunk = (2, n, rows, head)
    dma = pltpu.SemaphoreType.DMA
    scratch = [
        pltpu.VMEM((tokens, d_model), low),
        pltpu.VMEM((d_model, tokens), low),
        pltpu.VMEM((tokens, head), low),
        pltpu.VMEM((rows, head), wide),
        pltpu.VMEM((rows, head), wide),
        pltpu.VMEM((rows, head), wide),
        pltpu.VMEM((1, rows), wide),
        pltpu.VMEM((1, rows), wide),
        pltpu.VMEM((1, rows), wide),
        pltpu.VMEM((rows, head), wide),
        pltpu.VMEM((rows, head), wide),
        pltpu.VMEM((2, n, *chunk), low),
        pltpu.VMEM((2, n, *chunk), low),
        pltpu.VMEM((n, *chunk), low),
        pltpu.VMEM((plus, *chunk), low),
        pltpu.VMEM((minus, *chunk), low),
        pltpu.VMEM((plus, *chunk), low),
        pltpu.VMEM((minus, *chunk), low),
        pltpu.VMEM(chunk, low),
        pltpu.VMEM((n - 1, 2, rows, head), low),
        pltpu.VMEM((2, rows, head), wide),
        pltpu.VMEM((rows, head), wide),
        pltpu.VMEM((n_rep, rows, head), wide),
        dma((10,)),
        dma((2, n - 1)),
        dma((2, plus, SUBS)),
        dma((2, minus, SUBS)),
        dma((2, n)),
        dma((2, n)),
        dma((2, plus, SUBS)),
        dma((2, minus, SUBS)),
        dma((2, n - 1)),
        dma((2, 2)),
        dma((2, max(n_rep - 1, 1))),
    ]
    shape = jax.ShapeDtypeStruct
    return pl.pallas_call(
        functools.partial(kernel, n, n_rep),
        out_shape=(
            shape((1, rows, head), wide),
            shape((1, rows), wide),
            shape((rows, head), wide),
            shape((rows, head), wide),
        ),
        in_specs=[pl.BlockSpec(memory_space=pl.ANY)] * 10,
        out_specs=tuple([pl.BlockSpec(memory_space=pltpu.VMEM)] * 4),
        scratch_shapes=scratch,
        compiler_params=pltpu.CompilerParams(
            collective_id=0, has_side_effects=True, vmem_limit_bytes=48 * 1024 * 1024
        ),
        cost_estimate=pl.CostEstimate(
            flops=4 * tokens * d_model * head, bytes_accessed=2 * tokens * d_model, transcendentals=0
        ),
    )(*args)


def solution(mesh):
    return jax.shard_map(
        per_device,
        mesh=mesh,
        in_specs=(
            P("rep", "fsdp", None),
            P("rep", "fsdp", None),
            P("rep", "fsdp", None),
            P("rep", "fsdp", None),
            P("rep", "fsdp", None),
            P("rep", "fsdp"),
            P("rep", "fsdp"),
            P("rep", "fsdp"),
            P("fsdp", None),
            P("fsdp", None),
        ),
        out_specs=(P("rep", "fsdp", None), P("rep", "fsdp"), P("fsdp", None), P("fsdp", None)),
        check_vma=False,
    )
```

time: 2280 us -> 93.6 us (0.04)
  the two profiles are of different devices: /device:TPU:32 before, /device:TPU:16 now
where the time goes in v1:
time: 93.6 us; the launch traced here: 93 us
  Pallas kernels  81.7 us (87%)
  local copies, waits for them, and re-layouts  10.6 us (11%)
    pallas_call x1, Pallas kernels, per_device(): pl.pallas_call(functools.partial(kernel, n, n_rep), out_shape=(shape((1,...  81.7 us
    unnamed x24, local copies, waits for them, and re-layouts  10.6 us

profile of v1, /device:TPU:16, one launch (start us, length us, event | category | flops | bytes accessed | tf_op | source)
XLA Modules:
  0.0 93.0 jit_solution(13984195740439702528)
XLA Ops:
  0.6 0.0 copy-start
  0.6 1.9 %copy-done = bf16[1,192,8192]{2,1,0:T(8,128)(2,1)S(1)} copy-done((bf16[1,192,8192]{2,1,0:T(8,128)(2,1)S(1)}, bf16[1,192,8192]{2,1,0:T(8,128)(2,1)}, u32[]{:S(2)}) %copy-start) | copy-done | bytes 3145752
  2.5 0.0 copy-start.1
  2.5 0.8 copy-done.1
  3.3 0.0 copy-start.2
  3.3 0.7 copy-done.2
  4.0 0.0 copy-start.3
  4.0 0.7 copy-done.3
  4.8 0.0 copy-start.4
  4.8 0.7 copy-done.4
  5.5 0.0 copy-start.5
  5.5 0.7 copy-done.5
  6.2 0.0 copy-start.6
  6.2 0.7 copy-done.6
  6.9 0.0 copy-start.7
  6.9 0.7 copy-done.7
  7.6 0.0 copy-start.8
  7.6 0.7 copy-done.8
  8.2 0.7 copy-done.9
  8.9 81.7 %shard_map.129 = (f32[1,32,128]{2,1,0:T(8,128)S(1)}, f32[1,32]{1,0:T(1,128)S(1)}, f32[32,128]{1,0:T(8,128)S(1)}, f32[32,128]{1,0:T(8,128)S(1)}) custom-call(bf16[1,192,8192]{2,1,0:T(8,128)(2,1)S(1)} %copy-done, bf16[1,192,128]{2,1,0:T(8,128)(2,1)S(1)} %copy-done.1, f32[1,32,128]{2,1,0:T(8,128)S(1)} %copy-done.2, f32[1,32,128]{2,1,0:T(8,128)S(1)} %copy-done.3, ...), custom_call_target="tpu_custom_call" | custom-call | flops 805306368 | bytes 3145728 | tf_op jit(solution)/shard_map/pallas_call | solution.py:450
  90.6 0.6 copy.18
  91.2 0.5 copy.19
  91.7 0.6 copy.20
  92.3 0.6 copy.21
  (1 shorter events, 0.0 us)
Async XLA Ops:
  0.6 1.9 %copy-start = (bf16[1,192,8192]{2,1,0:T(8,128)(2,1)S(1)}, bf16[1,192,8192]{2,1,0:T(8,128)(2,1)}, u32[]{:S(2)}) copy-start(bf16[1,192,8192]{2,1,0:T(8,128)(2,1)} %acts_hbm.1) | copy-start | bytes 9437188
  2.5 0.8 copy-start.1
  3.3 0.7 copy-start.2
  4.0 0.7 copy-start.3
  4.8 0.7 copy-start.4
  5.5 0.7 copy-start.5
  6.2 0.7 copy-start.6
  6.9 0.7 copy-start.7
  7.6 0.7 copy-start.8
  8.2 0.7 copy-start.9

commit v2 on v1

v2 whole, which is shorter than its diff:
```python
import functools
import math

import jax
import jax.numpy as jnp
from jax import lax
from jax.experimental import pallas as pl
from jax.experimental.pallas import tpu as pltpu
from jax.sharding import PartitionSpec as P

MESH = pl.DeviceIdType.MESH

norm_eps = 1e-05
adam_eps = 1e-08
beta_first = 0.9
beta_second = 0.95
bias_first = 1.0 - 0.9**50
bias_second = 1.0 - 0.95**50
inner_rate = 0.1
decay_rate = 0.1
outer_rate = 0.7
nesterov = 0.9
mixing = 0.5

SUBS = 4


def adam_step(param, grad, first, second):
    first = beta_first * first + (1.0 - beta_first) * grad
    second = beta_second * second + (1.0 - beta_second) * grad * grad
    update = first / bias_first / (jnp.sqrt(second / bias_second) + adam_eps)
    return param - inner_rate * (update + decay_rate * param)


def kernel(
    n,
    n_rep,
    acts_hbm,
    targets_hbm,
    weight_hbm,
    first_hbm,
    second_hbm,
    gain_hbm,
    gain_first_hbm,
    gain_second_hbm,
    base_hbm,
    momentum_hbm,
    new_weight_ref,
    new_gain_ref,
    new_base_ref,
    new_momentum_ref,
    acts,
    acts_t,
    targets,
    weight,
    first,
    second,
    gain,
    gain_first,
    gain_second,
    base,
    momentum,
    full_w,
    grads,
    keys_t,
    from_core,
    out_far,
    out_three,
    out_two,
    out_one,
    in_far,
    in_three,
    in_two,
    in_one,
    mine,
    from_peers,
    drifts,
    sem_in,
    sem_peers,
    sem_big,
    sem_core,
    sem_rep,
):
    tokens, d_model = acts.shape
    rows = weight.shape[0]
    token_count = tokens * 4 * n * n
    root_scale = 1.0 / math.sqrt(d_model)

    rep = lax.axis_index("rep")
    f = lax.axis_index("fsdp")
    c = lax.rem(f, 2)
    x = lax.rem(lax.div(f, 2), n)
    y = lax.rem(lax.div(f, 2 * n), 2)
    z = lax.div(f, 4 * n)
    s = x * (1 - c) + z * c
    b = z * (1 - c) + x * c

    def wrap(v):
        return lax.rem(v + n, n)

    def dev(ss, bb, yy):
        xx = ss * (1 - c) + bb * c
        zz = bb * (1 - c) + ss * c
        return ((zz * 2 + yy) * n + xx) * 2 + c

    sibling = f + 1 - 2 * c
    up, down = dev(s, wrap(b + 1), y), dev(s, wrap(b - 1), y)
    up_two, down_two = dev(s, wrap(b + 2), y), dev(s, wrap(b - 2), y)

    def remote(src, dst, sems, target):
        return pltpu.make_async_remote_copy(
            src_ref=src,
            dst_ref=dst,
            send_sem=sems[0],
            recv_sem=sems[1],
            device_id={"fsdp": target},
            device_id_type=MESH,
        )

    def pair(sem, *at):
        return sem.at[(0, *at)], sem.at[(1, *at)]

    loads = [
        pltpu.make_async_copy(src, dst, sem_in.at[i])
        for i, (src, dst) in enumerate(
            [
                (weight_hbm.at[0], weight),
                (gain_hbm, gain),
                (acts_hbm.at[0], acts),
                (targets_hbm.at[0], targets),
                (first_hbm.at[0], first),
                (second_hbm.at[0], second),
                (gain_first_hbm, gain_first),
                (gain_second_hbm, gain_second),
                (base_hbm, base),
                (momentum_hbm, momentum),
            ]
        )
    ]
    loads[0].start()
    loads[1].start()

    peers = [(k, d) for k in (4, 3, 5, 2, 6, 1, 7, 0) for d in (1, 0) if k or d]
    barrier = pltpu.get_barrier_semaphore()
    greeted = [sibling, up, down, up_two, down_two]
    greeted += [dev(wrap(s + k), b, lax.rem(y + d, 2)) for k, d in peers]
    for target in greeted:
        pl.semaphore_signal(barrier, inc=1, device_id={"fsdp": target}, device_id_type=MESH)
    for k in range(1, n_rep):
        pl.semaphore_signal(
            barrier, inc=1, device_id={"rep": lax.rem(rep + k, n_rep)}, device_id_type=MESH
        )
    for load in loads[2:]:
        load.start()

    loads[0].wait()
    loads[1].wait()
    row_ids = lax.broadcasted_iota(jnp.int32, (rows, rows), 0)
    lane_ids = lax.broadcasted_iota(jnp.int32, (rows, rows), 1)
    eye = row_ids == lane_ids

    def to_column(row):
        return jnp.sum(jnp.where(eye, jnp.broadcast_to(row, (rows, rows)), 0.0), axis=1, keepdims=True)

    def to_row(column):
        return jnp.sum(jnp.where(eye, jnp.broadcast_to(column, (rows, rows)), 0.0), axis=0, keepdims=True)

    gain_used = to_column(gain[...].astype(jnp.bfloat16).astype(jnp.float32))
    low_weight = weight[...].astype(jnp.bfloat16).astype(jnp.float32)
    full_w[c, b, y, s] = (gain_used * low_weight).astype(jnp.bfloat16)
    pl.semaphore_wait(barrier, len(greeted) + n_rep - 1)

    own_rows = full_w.at[c, b, y, s]
    gather_peers = []
    for i, (k, d) in enumerate(peers):
        target = dev(wrap(s + k), b, lax.rem(y + d, 2))
        gather_peers.append(remote(own_rows, own_rows, pair(sem_peers, 0, i), target))
        gather_peers[-1].start()

    loads[2].wait()
    width = d_model // n

    def prepare(i, total):
        columns = pl.ds(pl.multiple_of(i * width, width), width)
        block = acts[:, columns]
        acts_t[i] = block.T.reshape(2, n, 2, rows, tokens)
        wide = block.astype(jnp.float32)
        square = wide * wide
        for j in range(width // 128):
            total = total + square[:, j * 128 : (j + 1) * 128]
        return total

    squares = lax.fori_loop(0, n, prepare, jnp.zeros((tokens, 128), jnp.float32))
    factor = lax.rsqrt(jnp.sum(squares, axis=1, keepdims=True) / d_model + norm_eps)
    keys_t[...] = jnp.zeros_like(keys_t)
    loads[3].wait()

    for i, (k, d) in enumerate(peers):
        landed = full_w.at[c, b, lax.rem(y + d, 2), wrap(s - k)]
        remote(landed, landed, pair(sem_peers, 0, i), sibling).wait_recv()

    half = n // 2

    def at(j):
        return (j // 2, pl.ds((j % 2) * half, half))

    def part(ref, j):
        return ref.at[at(j)]

    def big(phase, kind, src, dst, target, quarters=range(SUBS)):
        return [
            remote(part(src, j), part(dst, j), pair(sem_big, phase, kind, j), target)
            for j in quarters
        ]

    def gathered(offset):
        return full_w.at[c, wrap(b + offset)]

    def gather_core(i, owner, place):
        chunk = full_w.at[owner, wrap(place)]
        return remote(chunk, chunk, pair(sem_core, 0, i), sibling)

    def chunk_acts(owner, place):
        pieces = []
        for yy in range(2):
            for ss in range(n):
                zz = place * (1 - owner) + ss * owner
                xx = ss * (1 - owner) + place * owner
                pieces.append(acts_t[zz, yy, xx, owner])
        return jnp.concatenate(pieces, axis=0)

    deep = 2 * n * rows

    def forward(owner, place):
        place = wrap(place)
        keys_t[...] += lax.dot_general(
            full_w[owner, place].reshape(deep, 128),
            chunk_acts(owner, place),
            (((0,), (0,)), ((), ())),
            preferred_element_type=jnp.float32,
        )

    core_offsets = [0, -2, 2, -1, 1, -3, 3, -4]

    def send_core(i):
        gather_core(i, c, b + core_offsets[i]).start()

    def from_sibling(i):
        gather_core(i, 1 - c, s + core_offsets[i]).wait_recv()
        forward(1 - c, s + core_offsets[i])

    two_up = big(0, 0, gathered(0), gathered(0), up_two)
    two_down = big(0, 1, gathered(0), gathered(0), down_two)
    one_up = big(0, 2, gathered(0), gathered(0), up)
    one_down = big(0, 3, gathered(0), gathered(0), down)
    three_up = big(0, 4, gathered(-2), gathered(-2), up)
    three_down = big(0, 5, gathered(2), gathered(2), down)
    four_up = big(0, 6, gathered(-2), gathered(-2), up_two, range(2))
    four_down = big(0, 6, gathered(2), gathered(2), down_two, range(2, SUBS))
    two_up_in = big(0, 0, gathered(-2), gathered(-2), up_two)
    two_down_in = big(0, 1, gathered(2), gathered(2), down_two)
    one_up_in = big(0, 2, gathered(-1), gathered(-1), up)
    one_down_in = big(0, 3, gathered(1), gathered(1), down)
    three_up_in = big(0, 4, gathered(-3), gathered(-3), up)
    three_down_in = big(0, 5, gathered(3), gathered(3), down)
    four_in = big(0, 6, gathered(-4), gathered(-4), up_two)

    for j in range(SUBS):
        two_up[j].start()
        two_down[j].start()
    for j in range(SUBS):
        one_up[j].start()
        one_down[j].start()
    send_core(0)
    forward(c, b)
    for j in range(SUBS):
        two_up_in[j].wait_recv()
        if j < 2:
            four_up[j].start()
        three_up[j].start()
        two_down_in[j].wait_recv()
        if j >= 2:
            four_down[j - 2].start()
        three_down[j].start()
    send_core(1)
    send_core(2)
    from_sibling(0)
    for j in range(SUBS):
        one_up_in[j].wait_recv()
        one_down_in[j].wait_recv()
    send_core(3)
    send_core(4)
    for i in range(1, 5):
        forward(c, b + core_offsets[i])
    for i in range(1, 5):
        from_sibling(i)
    for j in range(SUBS):
        three_up_in[j].wait_recv()
        three_down_in[j].wait_recv()
    send_core(5)
    send_core(6)
    forward(c, b + core_offsets[5])
    forward(c, b + core_offsets[6])
    for j in range(SUBS):
        four_in[j].wait_recv()
    send_core(7)
    forward(c, b + core_offsets[7])
    for i in range(5, 8):
        from_sibling(i)

    residual = keys_t[...].T * factor * root_scale - targets[...].astype(jnp.float32)
    scaled = (residual * factor).astype(jnp.bfloat16)

    def backward(owner, place):
        place = wrap(place)
        block = jnp.dot(chunk_acts(owner, place), scaled, preferred_element_type=jnp.float32)
        grads[owner, place] = block.astype(jnp.bfloat16).reshape(2, n, rows, 128)

    offsets = [4, -3, 3, -1, 1, -2, 2, 0]

    def reduce_core(i, owner, place):
        chunk = wrap(place)
        return remote(grads.at[owner, chunk], from_core.at[chunk], pair(sem_core, 1, i), sibling)

    def own(offset, j):
        chunk = wrap(b + offset)
        return grads[(c, chunk, *at(j))].astype(jnp.float32) + from_core[
            (chunk, *at(j))
        ].astype(jnp.float32)

    far_down = big(1, 0, out_far, in_far, down_two, range(2))
    far_up = big(1, 0, out_far, in_far, up_two, range(2, SUBS))
    three = [
        big(1, 1, out_three.at[0], in_three.at[0], down),
        big(1, 2, out_three.at[1], in_three.at[1], up),
    ]
    one = [
        big(1, 3, out_one.at[0], in_one.at[0], down),
        big(1, 4, out_one.at[1], in_one.at[1], up),
    ]
    two = [
        big(1, 5, out_two.at[0], in_two.at[0], down_two),
        big(1, 6, out_two.at[1], in_two.at[1], up_two),
    ]
    far = far_down + far_up

    def pass_on(offset):
        i = offsets.index(offset)
        reduce_core(i, c, b + offset).wait_recv()
        side = int(offset > 0)
        for j in range(SUBS):
            value = own(offset, j)
            if abs(offset) == 2:
                three[side][j].wait_recv()
                value = value + in_three[(side, *at(j))].astype(jnp.float32)
                if j // 2 == side:
                    far[j].wait_recv()
                    value = value + in_far[at(j)].astype(jnp.float32)
            low = value.astype(jnp.bfloat16)
            if offset == 4:
                out_far[at(j)] = low
                far[j].start()
            else:
                box, copies = {3: (out_three, three), 2: (out_two, two), 1: (out_one, one)}[abs(offset)]
                box[(side, *at(j))] = low
                copies[side][j].start()

    lag = 2
    for i, offset in enumerate(offsets):
        backward(1 - c, s + offset)
        reduce_core(i, 1 - c, s + offset).start()
        backward(c, b + offset)
        if i >= lag:
            pass_on(offsets[i - lag])
    for offset in offsets[len(offsets) - lag : -1]:
        pass_on(offset)
    reduce_core(len(offsets) - 1, c, b).wait_recv()
    for j in range(SUBS):
        value = own(0, j)
        for box, copies in ((in_one, one), (in_two, two)):
            for side in range(2):
                copies[side][j].wait_recv()
                value = value + box[(side, *at(j))].astype(jnp.float32)
        mine[at(j)] = value.astype(jnp.bfloat16)

    reduce_peers = []
    for i, (k, d) in enumerate(peers):
        ss, yy = wrap(s + k), lax.rem(y + d, 2)
        reduce_peers.append(
            remote(mine.at[yy, ss], from_peers.at[i], pair(sem_peers, 1, i), dev(ss, b, yy))
        )
        reduce_peers[-1].start()
    for load in loads[4:]:
        load.wait()
    grad_sum = mine[y, s].astype(jnp.float32)
    for i, copy in enumerate(reduce_peers):
        copy.wait_recv()
        grad_sum = grad_sum + from_peers[i].astype(jnp.float32)

    grad_weight = gain_used * grad_sum * root_scale / token_count
    inner_weight = adam_step(weight[...], grad_weight, first[...], second[...])
    drifts[rep] = base[...] - inner_weight
    rep_copies = []
    for k in range(1, n_rep):
        rep_copies.append(
            pltpu.make_async_remote_copy(
                src_ref=drifts.at[rep],
                dst_ref=drifts.at[rep],
                send_sem=sem_rep.at[0, k - 1],
                recv_sem=sem_rep.at[1, k - 1],
                device_id={"rep": lax.rem(rep + k, n_rep)},
                device_id_type=MESH,
            )
        )
        rep_copies[-1].start()

    gain_sum = to_row(jnp.sum(grad_sum * low_weight, axis=1, keepdims=True) * root_scale)
    new_gain_ref[...] = adam_step(gain[...], gain_sum / token_count, gain_first[...], gain_second[...])

    for copy in rep_copies:
        copy.wait_recv()
    average = drifts[0]
    for k in range(1, n_rep):
        average = average + drifts[k]
    average = average / n_rep
    new_momentum = nesterov * momentum[...] + average
    new_base = base[...] - outer_rate * (average + nesterov * new_momentum)
    new_momentum_ref[...] = new_momentum
    new_base_ref[...] = new_base
    new_weight_ref[0] = mixing * inner_weight + (1.0 - mixing) * new_base

    for copy in gather_peers + reduce_peers + rep_copies:
        copy.wait_send()
    for copies in (two_up, two_down, one_up, one_down, three_up, three_down, four_up, four_down):
        for copy in copies:
            copy.wait_send()
    for copies in (far, *three, *two, *one):
        for copy in copies:
            copy.wait_send()
    for i, offset in enumerate(core_offsets):
        gather_core(i, c, b + offset).wait_send()
    for i, offset in enumerate(offsets):
        reduce_core(i, 1 - c, s + offset).wait_send()


def per_device(*args):
    acts, targets, weight, _, _, gain = args[:6]
    n_rep = lax.axis_size("rep")
    n = math.isqrt(lax.axis_size("fsdp") // 4)
    tokens, d_model = acts.shape[1:]
    rows, head = weight.shape[1:]
    low, wide = jnp.bfloat16, jnp.float32
    chunk = (2, n, rows, head)
    dma = pltpu.SemaphoreType.DMA
    scratch = [
        pltpu.VMEM((tokens, d_model), low),
        pltpu.VMEM((n, 2, n, 2, rows, tokens), low),
        pltpu.VMEM((tokens, head), low),
        pltpu.VMEM((rows, head), wide),
        pltpu.VMEM((rows, head), wide),
        pltpu.VMEM((rows, head), wide),
        pltpu.VMEM((1, rows), wide),
        pltpu.VMEM((1, rows), wide),
        pltpu.VMEM((1, rows), wide),
        pltpu.VMEM((rows, head), wide),
        pltpu.VMEM((rows, head), wide),
        pltpu.VMEM((2, n, *chunk), low),
        pltpu.VMEM((2, n, *chunk), low),
        pltpu.VMEM((head, tokens), wide),
        pltpu.VMEM((n, *chunk), low),
        pltpu.VMEM(chunk, low),
        pltpu.VMEM((2, *chunk), low),
        pltpu.VMEM((2, *chunk), low),
        pltpu.VMEM((2, *chunk), low),
        pltpu.VMEM(chunk, low),
        pltpu.VMEM((2, *chunk), low),
        pltpu.VMEM((2, *chunk), low),
        pltpu.VMEM((2, *chunk), low),
        pltpu.VMEM(chunk, low),
        pltpu.VMEM((2 * n - 1, rows, head), low),
        pltpu.VMEM((n_rep, rows, head), wide),
        dma((10,)),
        dma((2, 2, 2 * n - 1)),
        dma((2, 2, 7, SUBS)),
        dma((2, 2, n)),
        dma((2, max(n_rep - 1, 1))),
    ]
    shape = jax.ShapeDtypeStruct
    return pl.pallas_call(
        functools.partial(kernel, n, n_rep),
        out_shape=(
            shape((1, rows, head), wide),
            shape((1, rows), wide),
            shape((rows, head), wide),
            shape((rows, head), wide),
        ),
        in_specs=[pl.BlockSpec(memory_space=pltpu.HBM)] * 10,
        out_specs=tuple([pl.BlockSpec(memory_space=pltpu.VMEM)] * 4),
        scratch_shapes=scratch,
        compiler_params=pltpu.CompilerParams(
            collective_id=0, has_side_effects=True, vmem_limit_bytes=48 * 1024 * 1024
        ),
        cost_estimate=pl.CostEstimate(
            flops=4 * tokens * d_model * head, bytes_accessed=2 * tokens * d_model, transcendentals=0
        ),
    )(*args)


def solution(mesh):
    return jax.shard_map(
        per_device,
        mesh=mesh,
        in_specs=(
            P("rep", "fsdp", None),
            P("rep", "fsdp", None),
            P("rep", "fsdp", None),
            P("rep", "fsdp", None),
            P("rep", "fsdp", None),
            P("rep", "fsdp"),
            P("rep", "fsdp"),
            P("rep", "fsdp"),
            P("fsdp", None),
            P("fsdp", None),
        ),
        out_specs=(P("rep", "fsdp", None), P("rep", "fsdp"), P("fsdp", None), P("fsdp", None)),
        check_vma=False,
    )
```

time: 93.6 us -> 77.5 us (0.83)
  the two profiles are of different devices: /device:TPU:16 before, /device:TPU:2 now
where the time goes in v2:
time: 77.5 us; the launch traced here: 76.9 us
  Pallas kernels  65.7 us (85%)
  local copies, waits for them, and re-layouts  10.6 us (14%)
    pallas_call x1, Pallas kernels, per_device(): pl.pallas_call(functools.partial(kernel, n, n_rep), out_shape=(shape((1,...  65.7 us
    unnamed x24, local copies, waits for them, and re-layouts  10.6 us

profile of v2, /device:TPU:2, one launch (start us, length us, event | category | flops | bytes accessed | tf_op | source)
XLA Modules:
  0.0 76.9 jit_solution(4059417291288282764)
XLA Ops:
  0.6 0.0 copy-start
  0.6 1.9 %copy-done = bf16[1,192,8192]{2,1,0:T(8,128)(2,1)S(1)} copy-done((bf16[1,192,8192]{2,1,0:T(8,128)(2,1)S(1)}, bf16[1,192,8192]{2,1,0:T(8,128)(2,1)}, u32[]{:S(2)}) %copy-start) | copy-done | bytes 3145752
  2.5 0.0 copy-start.1
  2.5 0.8 %copy-done.1 = bf16[1,192,128]{2,1,0:T(8,128)(2,1)S(1)} copy-done((bf16[1,192,128]{2,1,0:T(8,128)(2,1)S(1)}, bf16[1,192,128]{2,1,0:T(8,128)(2,1)}, u32[]{:S(2)}) %copy-start.1) | copy-done | bytes 49176
  3.3 0.0 copy-start.2
  3.3 0.7 copy-done.2
  4.0 0.0 copy-start.3
  4.0 0.7 copy-done.3
  4.8 0.0 copy-start.4
  4.8 0.7 copy-done.4
  5.5 0.0 copy-start.5
  5.5 0.7 copy-done.5
  6.2 0.0 copy-start.6
  6.2 0.7 copy-done.6
  6.9 0.0 copy-start.7
  6.9 0.7 copy-done.7
  7.6 0.0 copy-start.8
  7.6 0.7 copy-done.8
  8.2 0.7 copy-done.9
  8.9 65.7 %shard_map.129 = (f32[1,32,128]{2,1,0:T(8,128)S(1)}, f32[1,32]{1,0:T(1,128)S(1)}, f32[32,128]{1,0:T(8,128)S(1)}, f32[32,128]{1,0:T(8,128)S(1)}) custom-call(bf16[1,192,8192]{2,1,0:T(8,128)(2,1)S(1)} %copy-done, bf16[1,192,128]{2,1,0:T(8,128)(2,1)S(1)} %copy-done.1, f32[1,32,128]{2,1,0:T(8,128)S(1)} %copy-done.2, f32[1,32,128]{2,1,0:T(8,128)S(1)} %copy-done.3, ...), custom_call_target="tpu_custom_call" | custom-call | flops 805306368 | bytes 3145728 | tf_op jit(solution)/shard_map/pallas_call | solution.py:489
  74.6 0.6 copy.18
  75.2 0.5 copy.19
  75.7 0.6 copy.20
  76.3 0.6 copy.21
  (1 shorter events, 0.0 us)
Async XLA Ops:
  0.6 1.9 %copy-start = (bf16[1,192,8192]{2,1,0:T(8,128)(2,1)S(1)}, bf16[1,192,8192]{2,1,0:T(8,128)(2,1)}, u32[]{:S(2)}) copy-start(bf16[1,192,8192]{2,1,0:T(8,128)(2,1)} %acts_hbm.1) | copy-start | bytes 9437188
  2.5 0.8 %copy-start.1 = (bf16[1,192,128]{2,1,0:T(8,128)(2,1)S(1)}, bf16[1,192,128]{2,1,0:T(8,128)(2,1)}, u32[]{:S(2)}) copy-start(bf16[1,192,128]{2,1,0:T(8,128)(2,1)} %targets_hbm.1) | copy-start | bytes 147460
  3.3 0.7 copy-start.2
  4.0 0.7 copy-start.3
  4.8 0.7 copy-start.4
  5.5 0.7 copy-start.5
  6.2 0.7 copy-start.6
  6.9 0.7 copy-start.7
  7.6 0.7 copy-start.8
  8.2 0.7 copy-start.9

commit v3 on v2

--- a/solution.py
+++ b/solution.py
@@ -23,6 +23,10 @@
 mixing = 0.5
 
 SUBS = 4
+PLACES = [(0, 0), (0, 1), (0, -1), (1, 0), (1, 1), (1, -1), (0, 2), (0, -2)]
+PLACES += [(1, 2), (1, -2), (0, 3), (0, -3), (1, 3), (1, -3), (0, 4), (1, 4)]
+MIRROR = [PLACES.index((d, k if k == 4 else -k)) for d, k in PLACES]
+FAR_UP, FAR_DOWN = (0, 2), (1, 3)
 
 
 def adam_step(param, grad, first, second):
@@ -44,11 +48,9 @@
     gain_first_hbm,
     gain_second_hbm,
     base_hbm,
-    momentum_hbm,
-    new_weight_ref,
+    inner_ref,
     new_gain_ref,
-    new_base_ref,
-    new_momentum_ref,
+    average_ref,
     acts,
     acts_t,
     targets,
@@ -59,7 +61,6 @@
     gain_first,
     gain_second,
     base,
-    momentum,
     full_w,
     grads,
     keys_t,
@@ -133,17 +134,19 @@
                 (gain_first_hbm, gain_first),
                 (gain_second_hbm, gain_second),
                 (base_hbm, base),
-                (momentum_hbm, momentum),
             ]
         )
     ]
     loads[0].start()
     loads[1].start()
 
-    peers = [(k, d) for k in (4, 3, 5, 2, 6, 1, 7, 0) for d in (1, 0) if k or d]
+    def peer(p):
+        d, k = PLACES[p]
+        return dev(wrap(s + k), b, lax.rem(y + d, 2))
+
     barrier = pltpu.get_barrier_semaphore()
     greeted = [sibling, up, down, up_two, down_two]
-    greeted += [dev(wrap(s + k), b, lax.rem(y + d, 2)) for k, d in peers]
+    greeted += [peer(p) for p in range(1, len(PLACES))]
     for target in greeted:
         pl.semaphore_signal(barrier, inc=1, device_id={"fsdp": target}, device_id_type=MESH)
     for k in range(1, n_rep):
@@ -167,15 +170,20 @@
 
     gain_used = to_column(gain[...].astype(jnp.bfloat16).astype(jnp.float32))
     low_weight = weight[...].astype(jnp.bfloat16).astype(jnp.float32)
-    full_w[c, b, y, s] = (gain_used * low_weight).astype(jnp.bfloat16)
+    full_w[c, b, 0] = (gain_used * low_weight).astype(jnp.bfloat16)
     pl.semaphore_wait(barrier, len(greeted) + n_rep - 1)
 
-    own_rows = full_w.at[c, b, y, s]
-    gather_peers = []
-    for i, (k, d) in enumerate(peers):
-        target = dev(wrap(s + k), b, lax.rem(y + d, 2))
-        gather_peers.append(remote(own_rows, own_rows, pair(sem_peers, 0, i), target))
-        gather_peers[-1].start()
+    gather_peers = [
+        remote(
+            full_w.at[c, b, 0],
+            full_w.at[c, b, MIRROR[p]],
+            (sem_peers.at[0, 0, p], sem_peers.at[1, 0, MIRROR[p]]),
+            peer(p),
+        )
+        for p in range(1, len(PLACES))
+    ]
+    for copy in reversed(gather_peers):
+        copy.start()
 
     loads[2].wait()
     width = d_model // n
@@ -195,14 +203,8 @@
     keys_t[...] = jnp.zeros_like(keys_t)
     loads[3].wait()
 
-    for i, (k, d) in enumerate(peers):
-        landed = full_w.at[c, b, lax.rem(y + d, 2), wrap(s - k)]
-        remote(landed, landed, pair(sem_peers, 0, i), sibling).wait_recv()
-
-    half = n // 2
-
     def at(j):
-        return (j // 2, pl.ds((j % 2) * half, half))
+        return (pl.ds(j * 4, 4),)
 
     def part(ref, j):
         return ref.at[at(j)]
@@ -220,34 +222,45 @@
         chunk = full_w.at[owner, wrap(place)]
         return remote(chunk, chunk, pair(sem_core, 0, i), sibling)
 
-    def chunk_acts(owner, place):
+    def chunk_acts(owner, small, place):
         pieces = []
-        for yy in range(2):
-            for ss in range(n):
-                zz = place * (1 - owner) + ss * owner
-                xx = ss * (1 - owner) + place * owner
-                pieces.append(acts_t[zz, yy, xx, owner])
+        for d, k in PLACES:
+            ss = wrap(small + k)
+            zz = place * (1 - owner) + ss * owner
+            xx = ss * (1 - owner) + place * owner
+            pieces.append(acts_t[zz, lax.rem(y + d, 2), xx, owner])
         return jnp.concatenate(pieces, axis=0)
 
     deep = 2 * n * rows
 
-    def forward(owner, place):
+    def forward(owner, small, place):
         place = wrap(place)
         keys_t[...] += lax.dot_general(
             full_w[owner, place].reshape(deep, 128),
-            chunk_acts(owner, place),
+            chunk_acts(owner, small, place),
             (((0,), (0,)), ((), ())),
             preferred_element_type=jnp.float32,
         )
 
     core_offsets = [0, -2, 2, -1, 1, -3, 3, -4]
 
+    def gather_core_last(j, owner, place):
+        quarter = part(full_w.at[owner, wrap(place)], j)
+        return remote(quarter, quarter, pair(sem_core, 0, n - 1 + j), sibling)
+
     def send_core(i):
         gather_core(i, c, b + core_offsets[i]).start()
 
     def from_sibling(i):
-        gather_core(i, 1 - c, s + core_offsets[i]).wait_recv()
-        forward(1 - c, s + core_offsets[i])
+        if i < n - 1:
+            gather_core(i, 1 - c, s + core_offsets[i]).wait_recv()
+        else:
+            for j in range(SUBS):
+                gather_core_last(j, 1 - c, s + core_offsets[i]).wait_recv()
+        forward(1 - c, b, s + core_offsets[i])
+
+    def forward_own(i):
+        forward(c, s, b + core_offsets[i])
 
     two_up = big(0, 0, gathered(0), gathered(0), up_two)
     two_down = big(0, 1, gathered(0), gathered(0), down_two)
@@ -255,8 +268,8 @@
     one_down = big(0, 3, gathered(0), gathered(0), down)
     three_up = big(0, 4, gathered(-2), gathered(-2), up)
     three_down = big(0, 5, gathered(2), gathered(2), down)
-    four_up = big(0, 6, gathered(-2), gathered(-2), up_two, range(2))
-    four_down = big(0, 6, gathered(2), gathered(2), down_two, range(2, SUBS))
+    four_up = big(0, 6, gathered(-2), gathered(-2), up_two, FAR_UP)
+    four_down = big(0, 6, gathered(2), gathered(2), down_two, FAR_DOWN)
     two_up_in = big(0, 0, gathered(-2), gathered(-2), up_two)
     two_down_in = big(0, 1, gathered(2), gathered(2), down_two)
     one_up_in = big(0, 2, gathered(-1), gathered(-1), up)
@@ -266,21 +279,23 @@
     four_in = big(0, 6, gathered(-4), gathered(-4), up_two)
 
     for j in range(SUBS):
+        for p in range(max(4 * j, 1), 4 * j + 4):
+            landed = full_w.at[c, b, p]
+            remote(landed, landed, pair(sem_peers, 0, p), sibling).wait_recv()
         two_up[j].start()
         two_down[j].start()
-    for j in range(SUBS):
         one_up[j].start()
         one_down[j].start()
     send_core(0)
-    forward(c, b)
+    forward_own(0)
     for j in range(SUBS):
         two_up_in[j].wait_recv()
-        if j < 2:
-            four_up[j].start()
+        if j in FAR_UP:
+            four_up[FAR_UP.index(j)].start()
         three_up[j].start()
         two_down_in[j].wait_recv()
-        if j >= 2:
-            four_down[j - 2].start()
+        if j in FAR_DOWN:
+            four_down[FAR_DOWN.index(j)].start()
         three_down[j].start()
     send_core(1)
     send_core(2)
@@ -291,7 +306,7 @@
     send_core(3)
     send_core(4)
     for i in range(1, 5):
-        forward(c, b + core_offsets[i])
+        forward_own(i)
     for i in range(1, 5):
         from_sibling(i)
     for j in range(SUBS):
@@ -299,22 +314,22 @@
         three_down_in[j].wait_recv()
     send_core(5)
     send_core(6)
-    forward(c, b + core_offsets[5])
-    forward(c, b + core_offsets[6])
+    forward_own(5)
+    forward_own(6)
     for j in range(SUBS):
         four_in[j].wait_recv()
-    send_core(7)
-    forward(c, b + core_offsets[7])
+        gather_core_last(j, c, b - 4).start()
+    forward_own(7)
     for i in range(5, 8):
         from_sibling(i)
 
     residual = keys_t[...].T * factor * root_scale - targets[...].astype(jnp.float32)
     scaled = (residual * factor).astype(jnp.bfloat16)
 
-    def backward(owner, place):
+    def backward(owner, small, place):
         place = wrap(place)
-        block = jnp.dot(chunk_acts(owner, place), scaled, preferred_element_type=jnp.float32)
-        grads[owner, place] = block.astype(jnp.bfloat16).reshape(2, n, rows, 128)
+        block = jnp.dot(chunk_acts(owner, small, place), scaled, preferred_element_type=jnp.float32)
+        grads[owner, place] = block.astype(jnp.bfloat16).reshape(2 * n, rows, 128)
 
     offsets = [4, -3, 3, -1, 1, -2, 2, 0]
 
@@ -328,8 +343,8 @@
             (chunk, *at(j))
         ].astype(jnp.float32)
 
-    far_down = big(1, 0, out_far, in_far, down_two, range(2))
-    far_up = big(1, 0, out_far, in_far, up_two, range(2, SUBS))
+    far_down = big(1, 0, out_far, in_far, down_two, FAR_DOWN)
+    far_up = big(1, 0, out_far, in_far, up_two, FAR_UP)
     three = [
         big(1, 1, out_three.at[0], in_three.at[0], down),
         big(1, 2, out_three.at[1], in_three.at[1], up),
@@ -342,18 +357,18 @@
         big(1, 5, out_two.at[0], in_two.at[0], down_two),
         big(1, 6, out_two.at[1], in_two.at[1], up_two),
     ]
-    far = far_down + far_up
+    far = {**dict(zip(FAR_DOWN, far_down)), **dict(zip(FAR_UP, far_up))}
 
     def pass_on(offset):
         i = offsets.index(offset)
         reduce_core(i, c, b + offset).wait_recv()
         side = int(offset > 0)
-        for j in range(SUBS):
+        for j in reversed(range(SUBS)):
             value = own(offset, j)
             if abs(offset) == 2:
                 three[side][j].wait_recv()
                 value = value + in_three[(side, *at(j))].astype(jnp.float32)
-                if j // 2 == side:
+                if j in (FAR_DOWN, FAR_UP)[side]:
                     far[j].wait_recv()
                     value = value + in_far[at(j)].astype(jnp.float32)
             low = value.astype(jnp.bfloat16)
@@ -367,35 +382,39 @@
 
     lag = 2
     for i, offset in enumerate(offsets):
-        backward(1 - c, s + offset)
+        backward(1 - c, b, s + offset)
         reduce_core(i, 1 - c, s + offset).start()
-        backward(c, b + offset)
+        backward(c, s, b + offset)
         if i >= lag:
             pass_on(offsets[i - lag])
     for offset in offsets[len(offsets) - lag : -1]:
         pass_on(offset)
     reduce_core(len(offsets) - 1, c, b).wait_recv()
-    for j in range(SUBS):
+
+    reduce_peers = [
+        remote(
+            mine.at[p],
+            from_peers.at[MIRROR[p]],
+            (sem_peers.at[0, 1, p], sem_peers.at[1, 1, MIRROR[p]]),
+            peer(p),
+        )
+        for p in range(1, len(PLACES))
+    ]
+    for j in reversed(range(SUBS)):
         value = own(0, j)
         for box, copies in ((in_one, one), (in_two, two)):
             for side in range(2):
                 copies[side][j].wait_recv()
                 value = value + box[(side, *at(j))].astype(jnp.float32)
         mine[at(j)] = value.astype(jnp.bfloat16)
-
-    reduce_peers = []
-    for i, (k, d) in enumerate(peers):
-        ss, yy = wrap(s + k), lax.rem(y + d, 2)
-        reduce_peers.append(
-            remote(mine.at[yy, ss], from_peers.at[i], pair(sem_peers, 1, i), dev(ss, b, yy))
-        )
-        reduce_peers[-1].start()
+        for p in reversed(range(max(4 * j, 1), 4 * j + 4)):
+            reduce_peers[p - 1].start()
     for load in loads[4:]:
         load.wait()
-    grad_sum = mine[y, s].astype(jnp.float32)
-    for i, copy in enumerate(reduce_peers):
-        copy.wait_recv()
-        grad_sum = grad_sum + from_peers[i].astype(jnp.float32)
+    grad_sum = mine[0].astype(jnp.float32)
+    for p in range(1, len(PLACES)):
+        remote(mine.at[p], from_peers.at[p], pair(sem_peers, 1, p), sibling).wait_recv()
+        grad_sum = grad_sum + from_peers[p].astype(jnp.float32)
 
     grad_weight = gain_used * grad_sum * root_scale / token_count
     inner_weight = adam_step(weight[...], grad_weight, first[...], second[...])
@@ -422,23 +441,21 @@
     average = drifts[0]
     for k in range(1, n_rep):
         average = average + drifts[k]
-    average = average / n_rep
-    new_momentum = nesterov * momentum[...] + average
-    new_base = base[...] - outer_rate * (average + nesterov * new_momentum)
-    new_momentum_ref[...] = new_momentum
-    new_base_ref[...] = new_base
-    new_weight_ref[0] = mixing * inner_weight + (1.0 - mixing) * new_base
+    average_ref[...] = average / n_rep
+    inner_ref[...] = inner_weight
 
     for copy in gather_peers + reduce_peers + rep_copies:
         copy.wait_send()
     for copies in (two_up, two_down, one_up, one_down, three_up, three_down, four_up, four_down):
         for copy in copies:
             copy.wait_send()
-    for copies in (far, *three, *two, *one):
+    for copies in (far.values(), *three, *two, *one):
         for copy in copies:
             copy.wait_send()
-    for i, offset in enumerate(core_offsets):
+    for i, offset in enumerate(core_offsets[:-1]):
         gather_core(i, c, b + offset).wait_send()
+    for j in range(SUBS):
+        gather_core_last(j, c, b - 4).wait_send()
     for i, offset in enumerate(offsets):
         reduce_core(i, 1 - c, s + offset).wait_send()
 
@@ -450,7 +467,7 @@
     tokens, d_model = acts.shape[1:]
     rows, head = weight.shape[1:]
     low, wide = jnp.bfloat16, jnp.float32
-    chunk = (2, n, rows, head)
+    chunk = (2 * n, rows, head)
     dma = pltpu.SemaphoreType.DMA
     scratch = [
         pltpu.VMEM((tokens, d_model), low),
@@ -462,7 +479,6 @@
         pltpu.VMEM((1, rows), wide),
         pltpu.VMEM((1, rows), wide),
         pltpu.VMEM((1, rows), wide),
-        pltpu.VMEM((rows, head), wide),
         pltpu.VMEM((rows, head), wide),
         pltpu.VMEM((2, n, *chunk), low),
         pltpu.VMEM((2, n, *chunk), low),
@@ -477,33 +493,37 @@
         pltpu.VMEM((2, *chunk), low),
         pltpu.VMEM((2, *chunk), low),
         pltpu.VMEM(chunk, low),
-        pltpu.VMEM((2 * n - 1, rows, head), low),
+        pltpu.VMEM((2 * n, rows, head), low),
         pltpu.VMEM((n_rep, rows, head), wide),
-        dma((10,)),
-        dma((2, 2, 2 * n - 1)),
+        dma((9,)),
+        dma((2, 2, 2 * n)),
         dma((2, 2, 7, SUBS)),
-        dma((2, 2, n)),
+        dma((2, 2, n + SUBS)),
         dma((2, max(n_rep - 1, 1))),
     ]
     shape = jax.ShapeDtypeStruct
-    return pl.pallas_call(
+    inner_weight, new_gain, average = pl.pallas_call(
         functools.partial(kernel, n, n_rep),
         out_shape=(
-            shape((1, rows, head), wide),
+            shape((rows, head), wide),
             shape((1, rows), wide),
             shape((rows, head), wide),
-            shape((rows, head), wide),
         ),
-        in_specs=[pl.BlockSpec(memory_space=pltpu.HBM)] * 10,
-        out_specs=tuple([pl.BlockSpec(memory_space=pltpu.VMEM)] * 4),
+        in_specs=[pl.BlockSpec(memory_space=pltpu.HBM)] * 9,
+        out_specs=tuple([pl.BlockSpec(memory_space=pltpu.VMEM)] * 3),
         scratch_shapes=scratch,
         compiler_params=pltpu.CompilerParams(
-            collective_id=0, has_side_effects=True, vmem_limit_bytes=48 * 1024 * 1024
+            collective_id=0, has_side_effects=True, vmem_limit_bytes=64 * 1024 * 1024
         ),
         cost_estimate=pl.CostEstimate(
             flops=4 * tokens * d_model * head, bytes_accessed=2 * tokens * d_model, transcendentals=0
         ),
-    )(*args)
+    )(*args[:-1])
+    base, momentum = args[-2:]
+    new_momentum = nesterov * momentum + average
+    new_base = base - outer_rate * (average + nesterov * new_momentum)
+    new_weight = mixing * inner_weight + (1.0 - mixing) * new_base
+    return new_weight[None], new_gain, new_base, new_momentum
 
 
 def solution(mesh):

time: 77.5 us -> 70.5 us (0.910)
  local copies, waits for them, and re-layouts: 10.6 us -> 1.14 us
  other arithmetic: 0 us -> 1.39 us
  Pallas kernels: 65.7 us -> 67 us
    unnamed x24 -> x1, local copies, waits for them, and re-layouts: 10.6 us -> 1.14 us
    broadcast_in_dim x0 -> x1, other arithmetic: none -> 1.39 us  [per_device(): return (new_weight[None], new_gain, new_base, new_momentum)]
    pallas_call x1, Pallas kernels: 65.7 us -> 67 us  [per_device(): pl.pallas_call(functools.partial(kernel, n, n_rep), out_shape=(shape((row...]
where the time goes in v3:
time: 70.5 us; the launch traced here: 70.2 us
  Pallas kernels  67 us (95%)
  other arithmetic  1.39 us (2%)
  local copies, waits for them, and re-layouts  1.14 us (2%)
    pallas_call x1, Pallas kernels, per_device(): pl.pallas_call(functools.partial(kernel, n, n_rep), out_shape=(shape((row...  67 us

profile of v3, /device:TPU:2, one launch (start us, length us, event | category | flops | bytes accessed | tf_op | source)
XLA Modules:
  0.0 70.2 jit_solution(16193468995018196501)
XLA Ops:
  0.6 67.0 %shard_map.129 = (f32[32,128]{1,0:T(8,128)}, f32[1,32]{1,0:T(1,128)}, f32[32,128]{1,0:T(8,128)}) custom-call(bf16[1,192,8192]{2,1,0:T(8,128)(2,1)} %acts_hbm.1, bf16[1,192,128]{2,1,0:T(8,128)(2,1)} %targets_hbm.1, f32[1,32,128]{2,1,0:T(8,128)} %weight_hbm.1, f32[1,32,128]{2,1,0:T(8,128)} %first_hbm.1, f32[1,32,128]{2,1,0:T(8,128)} %second_hbm.1, ...), custom_call_target="tpu_custom_call" | custom-call | flops 805306368 | bytes 3145728 | tf_op jit(solution)/shard_map/pallas_call | solution.py:505
  67.6 1.4 %multiply_bitcast_fusion = (f32[1,32,128]{2,1,0:T(8,128)}, f32[32,128]{1,0:T(8,128)}, f32[32,128]{1,0:T(8,128)}) fusion(f32[32,128]{1,0:T(8,128)} %get-tuple-element.7, f32[32,128]{1,0:T(8,128)} %base_hbm.1, f32[32,128]{1,0:T(8,128)} %get-tuple-element.8, f32[32,128]{1,0:T(8,128)} %param.19), kind=kLoop, calls=%fused_computation | loop fusion | flops 32768 | bytes 114688 | tf_op jit(solution)/shard_map/broadcast_in_dim | solution.py:526
  69.0 1.1 %copy.15 = f32[1,32]{1,0:T(1,128)} copy(f32[1,32]{1,0:T(1,128)} %get-tuple-element.18) | data formatting | bytes 256

commit v4 on v3

--- a/solution.py
+++ b/solution.py
@@ -96,8 +96,9 @@
     s = x * (1 - c) + z * c
     b = z * (1 - c) + x * c
 
-    def wrap(v):
-        return lax.rem(v + n, n)
+    small_at = {k: lax.rem(s + n + k, n) for k in range(-4, 5)}
+    big_at = {k: lax.rem(b + n + k, n) for k in range(-4, 5)}
+    y_at = (y, 1 - y)
 
     def dev(ss, bb, yy):
         xx = ss * (1 - c) + bb * c
@@ -105,8 +106,8 @@
         return ((zz * 2 + yy) * n + xx) * 2 + c
 
     sibling = f + 1 - 2 * c
-    up, down = dev(s, wrap(b + 1), y), dev(s, wrap(b - 1), y)
-    up_two, down_two = dev(s, wrap(b + 2), y), dev(s, wrap(b - 2), y)
+    up, down = dev(s, big_at[1], y), dev(s, big_at[-1], y)
+    up_two, down_two = dev(s, big_at[2], y), dev(s, big_at[-2], y)
 
     def remote(src, dst, sems, target):
         return pltpu.make_async_remote_copy(
@@ -117,6 +118,12 @@
             device_id={"fsdp": target},
             device_id_type=MESH,
         )
+
+    started = []
+
+    def go(copy):
+        copy.start()
+        started.append(copy)
 
     def pair(sem, *at):
         return sem.at[(0, *at)], sem.at[(1, *at)]
@@ -140,19 +147,14 @@
     loads[0].start()
     loads[1].start()
 
-    def peer(p):
-        d, k = PLACES[p]
-        return dev(wrap(s + k), b, lax.rem(y + d, 2))
+    peers = [dev(small_at[k], b, y_at[d]) for d, k in PLACES]
 
     barrier = pltpu.get_barrier_semaphore()
-    greeted = [sibling, up, down, up_two, down_two]
-    greeted += [peer(p) for p in range(1, len(PLACES))]
+    greeted = [{"rep": lax.rem(rep + k, n_rep)} for k in range(1, n_rep)]
+    nearby = peers[:0:-1] + [up_two, down_two, up, down, sibling]
+    greeted += [{"fsdp": target} for target in nearby]
     for target in greeted:
-        pl.semaphore_signal(barrier, inc=1, device_id={"fsdp": target}, device_id_type=MESH)
-    for k in range(1, n_rep):
-        pl.semaphore_signal(
-            barrier, inc=1, device_id={"rep": lax.rem(rep + k, n_rep)}, device_id_type=MESH
-        )
+        pl.semaphore_signal(barrier, inc=1, device_id=target, device_id_type=MESH)
     for load in loads[2:]:
         load.start()
 
@@ -171,19 +173,19 @@
     gain_used = to_column(gain[...].astype(jnp.bfloat16).astype(jnp.float32))
     low_weight = weight[...].astype(jnp.bfloat16).astype(jnp.float32)
     full_w[c, b, 0] = (gain_used * low_weight).astype(jnp.bfloat16)
-    pl.semaphore_wait(barrier, len(greeted) + n_rep - 1)
+    pl.semaphore_wait(barrier, len(greeted))
 
     gather_peers = [
         remote(
             full_w.at[c, b, 0],
             full_w.at[c, b, MIRROR[p]],
             (sem_peers.at[0, 0, p], sem_peers.at[1, 0, MIRROR[p]]),
-            peer(p),
+            peers[p],
         )
         for p in range(1, len(PLACES))
     ]
     for copy in reversed(gather_peers):
-        copy.start()
+        go(copy)
 
     loads[2].wait()
     width = d_model // n
@@ -216,25 +218,23 @@
         ]
 
     def gathered(offset):
-        return full_w.at[c, wrap(b + offset)]
+        return full_w.at[c, big_at[offset]]
 
     def gather_core(i, owner, place):
-        chunk = full_w.at[owner, wrap(place)]
+        chunk = full_w.at[owner, place]
         return remote(chunk, chunk, pair(sem_core, 0, i), sibling)
 
     def chunk_acts(owner, small, place):
         pieces = []
         for d, k in PLACES:
-            ss = wrap(small + k)
-            zz = place * (1 - owner) + ss * owner
-            xx = ss * (1 - owner) + place * owner
-            pieces.append(acts_t[zz, lax.rem(y + d, 2), xx, owner])
+            zz = place * (1 - owner) + small[k] * owner
+            xx = small[k] * (1 - owner) + place * owner
+            pieces.append(acts_t[zz, y_at[d], xx, owner])
         return jnp.concatenate(pieces, axis=0)
 
     deep = 2 * n * rows
 
     def forward(owner, small, place):
-        place = wrap(place)
         keys_t[...] += lax.dot_general(
             full_w[owner, place].reshape(deep, 128),
             chunk_acts(owner, small, place),
@@ -245,22 +245,22 @@
     core_offsets = [0, -2, 2, -1, 1, -3, 3, -4]
 
     def gather_core_last(j, owner, place):
-        quarter = part(full_w.at[owner, wrap(place)], j)
+        quarter = part(full_w.at[owner, place], j)
         return remote(quarter, quarter, pair(sem_core, 0, n - 1 + j), sibling)
 
     def send_core(i):
-        gather_core(i, c, b + core_offsets[i]).start()
+        go(gather_core(i, c, big_at[core_offsets[i]]))
 
     def from_sibling(i):
         if i < n - 1:
-            gather_core(i, 1 - c, s + core_offsets[i]).wait_recv()
+            gather_core(i, 1 - c, small_at[core_offsets[i]]).wait_recv()
         else:
             for j in range(SUBS):
-                gather_core_last(j, 1 - c, s + core_offsets[i]).wait_recv()
-        forward(1 - c, b, s + core_offsets[i])
+                gather_core_last(j, 1 - c, small_at[core_offsets[i]]).wait_recv()
+        forward(1 - c, big_at, small_at[core_offsets[i]])
 
     def forward_own(i):
-        forward(c, s, b + core_offsets[i])
+        forward(c, small_at, big_at[core_offsets[i]])
 
     two_up = big(0, 0, gathered(0), gathered(0), up_two)
     two_down = big(0, 1, gathered(0), gathered(0), down_two)
@@ -282,21 +282,21 @@
         for p in range(max(4 * j, 1), 4 * j + 4):
             landed = full_w.at[c, b, p]
             remote(landed, landed, pair(sem_peers, 0, p), sibling).wait_recv()
-        two_up[j].start()
-        two_down[j].start()
-        one_up[j].start()
-        one_down[j].start()
+        go(two_up[j])
+        go(two_down[j])
+        go(one_up[j])
+        go(one_down[j])
     send_core(0)
     forward_own(0)
     for j in range(SUBS):
         two_up_in[j].wait_recv()
         if j in FAR_UP:
-            four_up[FAR_UP.index(j)].start()
-        three_up[j].start()
+            go(four_up[FAR_UP.index(j)])
+        go(three_up[j])
         two_down_in[j].wait_recv()
         if j in FAR_DOWN:
-            four_down[FAR_DOWN.index(j)].start()
-        three_down[j].start()
+            go(four_down[FAR_DOWN.index(j)])
+        go(three_down[j])
     send_core(1)
     send_core(2)
     from_sibling(0)
@@ -318,7 +318,7 @@
     forward_own(6)
     for j in range(SUBS):
         four_in[j].wait_recv()
-        gather_core_last(j, c, b - 4).start()
+        go(gather_core_last(j, c, big_at[-4]))
     forward_own(7)
     for i in range(5, 8):
         from_sibling(i)
@@ -327,18 +327,16 @@
     scaled = (residual * factor).astype(jnp.bfloat16)
 
     def backward(owner, small, place):
-        place = wrap(place)
         block = jnp.dot(chunk_acts(owner, small, place), scaled, preferred_element_type=jnp.float32)
         grads[owner, place] = block.astype(jnp.bfloat16).reshape(2 * n, rows, 128)
 
     offsets = [4, -3, 3, -1, 1, -2, 2, 0]
 
     def reduce_core(i, owner, place):
-        chunk = wrap(place)
-        return remote(grads.at[owner, chunk], from_core.at[chunk], pair(sem_core, 1, i), sibling)
+        return remote(grads.at[owner, place], from_core.at[place], pair(sem_core, 1, i), sibling)
 
     def own(offset, j):
-        chunk = wrap(b + offset)
+        chunk = big_at[offset]
         return grads[(c, chunk, *at(j))].astype(jnp.float32) + from_core[
             (chunk, *at(j))
         ].astype(jnp.float32)
@@ -359,36 +357,35 @@
     ]
     far = {**dict(zip(FAR_DOWN, far_down)), **dict(zip(FAR_UP, far_up))}
 
-    def pass_on(offset):
-        i = offsets.index(offset)
-        reduce_core(i, c, b + offset).wait_recv()
-        side = int(offset > 0)
+    def pass_on(*group):
+        for offset in group:
+            reduce_core(offsets.index(offset), c, big_at[offset]).wait_recv()
         for j in reversed(range(SUBS)):
-            value = own(offset, j)
-            if abs(offset) == 2:
-                three[side][j].wait_recv()
-                value = value + in_three[(side, *at(j))].astype(jnp.float32)
-                if j in (FAR_DOWN, FAR_UP)[side]:
-                    far[j].wait_recv()
-                    value = value + in_far[at(j)].astype(jnp.float32)
-            low = value.astype(jnp.bfloat16)
-            if offset == 4:
-                out_far[at(j)] = low
-                far[j].start()
-            else:
-                box, copies = {3: (out_three, three), 2: (out_two, two), 1: (out_one, one)}[abs(offset)]
-                box[(side, *at(j))] = low
-                copies[side][j].start()
-
-    lag = 2
+            for offset in group:
+                side = int(offset > 0)
+                value = own(offset, j)
+                if abs(offset) == 2:
+                    three[side][j].wait_recv()
+                    value = value + in_three[(side, *at(j))].astype(jnp.float32)
+                    if j in (FAR_DOWN, FAR_UP)[side]:
+                        far[j].wait_recv()
+                        value = value + in_far[at(j)].astype(jnp.float32)
+                low = value.astype(jnp.bfloat16)
+                if offset == 4:
+                    out_far[at(j)] = low
+                    go(far[j])
+                else:
+                    box, copies = {3: (out_three, three), 2: (out_two, two), 1: (out_one, one)}[abs(offset)]
+                    box[(side, *at(j))] = low
+                    go(copies[side][j])
+
     for i, offset in enumerate(offsets):
-        backward(1 - c, b, s + offset)
-        reduce_core(i, 1 - c, s + offset).start()
-        backward(c, s, b + offset)
-        if i >= lag:
-            pass_on(offsets[i - lag])
-    for offset in offsets[len(offsets) - lag : -1]:
-        pass_on(offset)
+        backward(1 - c, big_at, small_at[offset])
+        go(reduce_core(i, 1 - c, small_at[offset]))
+        backward(c, small_at, big_at[offset])
+        if 2 <= i < 7:
+            pass_on(offsets[i - 2])
+    pass_on(-2, 2)
     reduce_core(len(offsets) - 1, c, b).wait_recv()
 
     reduce_peers = [
@@ -396,7 +393,7 @@
             mine.at[p],
             from_peers.at[MIRROR[p]],
             (sem_peers.at[0, 1, p], sem_peers.at[1, 1, MIRROR[p]]),
-            peer(p),
+            peers[p],
         )
         for p in range(1, len(PLACES))
     ]
@@ -408,7 +405,7 @@
                 value = value + box[(side, *at(j))].astype(jnp.float32)
         mine[at(j)] = value.astype(jnp.bfloat16)
         for p in reversed(range(max(4 * j, 1), 4 * j + 4)):
-            reduce_peers[p - 1].start()
+            go(reduce_peers[p - 1])
     for load in loads[4:]:
         load.wait()
     grad_sum = mine[0].astype(jnp.float32)
@@ -431,7 +428,7 @@
                 device_id_type=MESH,
             )
         )
-        rep_copies[-1].start()
+        go(rep_copies[-1])
 
     gain_sum = to_row(jnp.sum(grad_sum * low_weight, axis=1, keepdims=True) * root_scale)
     new_gain_ref[...] = adam_step(gain[...], gain_sum / token_count, gain_first[...], gain_second[...])
@@ -444,20 +441,8 @@
     average_ref[...] = average / n_rep
     inner_ref[...] = inner_weight
 
-    for copy in gather_peers + reduce_peers + rep_copies:
+    for copy in started:
         copy.wait_send()
-    for copies in (two_up, two_down, one_up, one_down, three_up, three_down, four_up, four_down):
-        for copy in copies:
-            copy.wait_send()
-    for copies in (far.values(), *three, *two, *one):
-        for copy in copies:
-            copy.wait_send()
-    for i, offset in enumerate(core_offsets[:-1]):
-        gather_core(i, c, b + offset).wait_send()
-    for j in range(SUBS):
-        gather_core_last(j, c, b - 4).wait_send()
-    for i, offset in enumerate(offsets):
-        reduce_core(i, 1 - c, s + offset).wait_send()
 
 
 def per_device(*args):
@@ -501,24 +486,23 @@
         dma((2, 2, n + SUBS)),
         dma((2, max(n_rep - 1, 1))),
     ]
-    shape = jax.ShapeDtypeStruct
     inner_weight, new_gain, average = pl.pallas_call(
         functools.partial(kernel, n, n_rep),
         out_shape=(
-            shape((rows, head), wide),
-            shape((1, rows), wide),
-            shape((rows, head), wide),
+            pltpu.VMEM((rows, head), wide),
+            pltpu.VMEM((1, rows), wide),
+            pltpu.VMEM((rows, head), wide),
         ),
         in_specs=[pl.BlockSpec(memory_space=pltpu.HBM)] * 9,
         out_specs=tuple([pl.BlockSpec(memory_space=pltpu.VMEM)] * 3),
         scratch_shapes=scratch,
         compiler_params=pltpu.CompilerParams(
-            collective_id=0, has_side_effects=True, vmem_limit_bytes=64 * 1024 * 1024
+            collective_id=0, has_side_effects=True, vmem_limit_bytes=48 * 1024 * 1024
         ),
         cost_estimate=pl.CostEstimate(
             flops=4 * tokens * d_model * head, bytes_accessed=2 * tokens * d_model, transcendentals=0
         ),
-    )(*args[:-1])
+    )(*[pltpu.with_memory_space_constraint(arg, pltpu.HBM) for arg in args[:-1]])
     base, momentum = args[-2:]
     new_momentum = nesterov * momentum + average
     new_base = base - outer_rate * (average + nesterov * new_momentum)

time: 70.5 us -> 66.9 us (0.949)
  the two profiles are of different devices: /device:TPU:2 before, /device:TPU:16 now
where the time goes in v4:
time: 66.9 us; the launch traced here: 66.7 us
  Pallas kernels  64.9 us (97%)
    pallas_call x1, Pallas kernels, per_device(): pl.pallas_call(functools.partial(kernel, n, n_rep), out_shape=(pltpu.VMEM...  64.9 us

profile of v4, /device:TPU:16, one launch (start us, length us, event | category | flops | bytes accessed | tf_op | source)
XLA Modules:
  0.0 66.7 jit_solution(6379850728472943022)
XLA Ops:
  0.6 0.0 copy-start
  0.6 0.0 copy-start.1
  0.7 64.9 %shard_map.129 = (f32[32,128]{1,0:T(8,128)S(1)}, f32[1,32]{1,0:T(1,128)S(1)}, f32[32,128]{1,0:T(8,128)S(1)}) custom-call(bf16[1,192,8192]{2,1,0:T(8,128)(2,1)} %acts_hbm.1, bf16[1,192,128]{2,1,0:T(8,128)(2,1)} %targets_hbm.1, f32[1,32,128]{2,1,0:T(8,128)} %weight_hbm.1, f32[1,32,128]{2,1,0:T(8,128)} %first_hbm.1, f32[1,32,128]{2,1,0:T(8,128)} %second_hbm.1, ...), custom_call_target="tpu_custom_call" | custom-call | flops 805306368 | bytes 3145728 | tf_op jit(solution)/shard_map/pallas_call | solution.py:489
  65.6 0.5 copy.15
  66.1 0.0 copy-done
  66.1 0.0 copy-done.1
  66.1 0.6 multiply_bitcast_fusion
Async XLA Ops:
  0.6 65.4 %copy-start = (f32[32,128]{1,0:T(8,128)S(1)}, f32[32,128]{1,0:T(8,128)}, u32[]{:S(2)}) copy-start(f32[32,128]{1,0:T(8,128)} %base_hbm.1) | copy-start | bytes 49156
  0.6 65.4 %copy-start.1 = (f32[32,128]{1,0:T(8,128)S(1)}, f32[32,128]{1,0:T(8,128)}, u32[]{:S(2)}) copy-start(f32[32,128]{1,0:T(8,128)} %param.19) | copy-start | bytes 49156

commit v5 on v4

--- a/solution.py
+++ b/solution.py
@@ -77,6 +77,7 @@
     from_peers,
     drifts,
     sem_in,
+    sem_send,
     sem_peers,
     sem_big,
     sem_core,
@@ -118,15 +119,6 @@
             device_id={"fsdp": target},
             device_id_type=MESH,
         )
-
-    started = []
-
-    def go(copy):
-        copy.start()
-        started.append(copy)
-
-    def pair(sem, *at):
-        return sem.at[(0, *at)], sem.at[(1, *at)]
 
     loads = [
         pltpu.make_async_copy(src, dst, sem_in.at[i])
@@ -179,13 +171,13 @@
         remote(
             full_w.at[c, b, 0],
             full_w.at[c, b, MIRROR[p]],
-            (sem_peers.at[0, 0, p], sem_peers.at[1, 0, MIRROR[p]]),
+            (sem_send.at[0], sem_peers.at[MIRROR[p] // 4]),
             peers[p],
         )
         for p in range(1, len(PLACES))
     ]
     for copy in reversed(gather_peers):
-        go(copy)
+        copy.start()
 
     loads[2].wait()
     width = d_model // n
@@ -211,18 +203,29 @@
     def part(ref, j):
         return ref.at[at(j)]
 
-    def big(phase, kind, src, dst, target, quarters=range(SUBS)):
+    def big(step, slot, src, dst, target, quarters=range(SUBS), each=True):
         return [
-            remote(part(src, j), part(dst, j), pair(sem_big, phase, kind, j), target)
+            remote(
+                part(src, j),
+                part(dst, j),
+                (sem_send.at[step], sem_big.at[slot + (j if each else 0)]),
+                target,
+            )
             for j in quarters
         ]
 
+    def landed(dst, sem):
+        remote(dst, dst, (sem_send.at[0], sem), sibling).wait_recv()
+
+    def sent(src, step):
+        remote(src, src, (sem_send.at[step], sem_big.at[0]), sibling).wait_send()
+
     def gathered(offset):
         return full_w.at[c, big_at[offset]]
 
     def gather_core(i, owner, place):
         chunk = full_w.at[owner, place]
-        return remote(chunk, chunk, pair(sem_core, 0, i), sibling)
+        return remote(chunk, chunk, (sem_send.at[2], sem_core.at[0, i]), sibling)
 
     def chunk_acts(owner, small, place):
         pieces = []
@@ -246,79 +249,68 @@
 
     def gather_core_last(j, owner, place):
         quarter = part(full_w.at[owner, place], j)
-        return remote(quarter, quarter, pair(sem_core, 0, n - 1 + j), sibling)
+        return remote(quarter, quarter, (sem_send.at[2], sem_core.at[0, n - 1]), sibling)
 
     def send_core(i):
-        go(gather_core(i, c, big_at[core_offsets[i]]))
+        gather_core(i, c, big_at[core_offsets[i]]).start()
 
     def from_sibling(i):
-        if i < n - 1:
-            gather_core(i, 1 - c, small_at[core_offsets[i]]).wait_recv()
-        else:
-            for j in range(SUBS):
-                gather_core_last(j, 1 - c, small_at[core_offsets[i]]).wait_recv()
+        gather_core(i, 1 - c, small_at[core_offsets[i]]).wait_recv()
         forward(1 - c, big_at, small_at[core_offsets[i]])
 
     def forward_own(i):
         forward(c, small_at, big_at[core_offsets[i]])
 
-    two_up = big(0, 0, gathered(0), gathered(0), up_two)
-    two_down = big(0, 1, gathered(0), gathered(0), down_two)
-    one_up = big(0, 2, gathered(0), gathered(0), up)
-    one_down = big(0, 3, gathered(0), gathered(0), down)
-    three_up = big(0, 4, gathered(-2), gathered(-2), up)
-    three_down = big(0, 5, gathered(2), gathered(2), down)
-    four_up = big(0, 6, gathered(-2), gathered(-2), up_two, FAR_UP)
-    four_down = big(0, 6, gathered(2), gathered(2), down_two, FAR_DOWN)
-    two_up_in = big(0, 0, gathered(-2), gathered(-2), up_two)
-    two_down_in = big(0, 1, gathered(2), gathered(2), down_two)
-    one_up_in = big(0, 2, gathered(-1), gathered(-1), up)
-    one_down_in = big(0, 3, gathered(1), gathered(1), down)
-    three_up_in = big(0, 4, gathered(-3), gathered(-3), up)
-    three_down_in = big(0, 5, gathered(3), gathered(3), down)
-    four_in = big(0, 6, gathered(-4), gathered(-4), up_two)
+    two_up = big(1, 0, gathered(0), gathered(0), up_two)
+    two_down = big(1, 4, gathered(0), gathered(0), down_two)
+    one_up = big(1, 8, gathered(0), gathered(0), up, each=False)
+    one_down = big(1, 9, gathered(0), gathered(0), down, each=False)
+    three_up = big(1, 10, gathered(-2), gathered(-2), up, each=False)
+    three_down = big(1, 11, gathered(2), gathered(2), down, each=False)
+    four_up = big(1, 12, gathered(-2), gathered(-2), up_two, FAR_UP)
+    four_down = big(1, 12, gathered(2), gathered(2), down_two, FAR_DOWN)
+    two_up_in = big(1, 0, gathered(-2), gathered(-2), up_two)
+    two_down_in = big(1, 4, gathered(2), gathered(2), down_two)
+    four_in = big(1, 12, gathered(-4), gathered(-4), up_two)
 
     for j in range(SUBS):
-        for p in range(max(4 * j, 1), 4 * j + 4):
-            landed = full_w.at[c, b, p]
-            remote(landed, landed, pair(sem_peers, 0, p), sibling).wait_recv()
-        go(two_up[j])
-        go(two_down[j])
-        go(one_up[j])
-        go(one_down[j])
+        first_row = max(4 * j, 1)
+        landed(full_w.at[c, b, pl.ds(first_row, 4 * j + 4 - first_row)], sem_peers.at[j])
+        two_up[j].start()
+        two_down[j].start()
+        one_up[j].start()
+        one_down[j].start()
     send_core(0)
     forward_own(0)
     for j in range(SUBS):
         two_up_in[j].wait_recv()
         if j in FAR_UP:
-            go(four_up[FAR_UP.index(j)])
-        go(three_up[j])
+            four_up[FAR_UP.index(j)].start()
+        three_up[j].start()
         two_down_in[j].wait_recv()
         if j in FAR_DOWN:
-            go(four_down[FAR_DOWN.index(j)])
-        go(three_down[j])
+            four_down[FAR_DOWN.index(j)].start()
+        three_down[j].start()
     send_core(1)
     send_core(2)
     from_sibling(0)
-    for j in range(SUBS):
-        one_up_in[j].wait_recv()
-        one_down_in[j].wait_recv()
+    landed(gathered(-1), sem_big.at[8])
+    landed(gathered(1), sem_big.at[9])
     send_core(3)
     send_core(4)
     for i in range(1, 5):
         forward_own(i)
     for i in range(1, 5):
         from_sibling(i)
-    for j in range(SUBS):
-        three_up_in[j].wait_recv()
-        three_down_in[j].wait_recv()
+    landed(gathered(-3), sem_big.at[10])
+    landed(gathered(3), sem_big.at[11])
     send_core(5)
     send_core(6)
     forward_own(5)
     forward_own(6)
     for j in range(SUBS):
         four_in[j].wait_recv()
-        go(gather_core_last(j, c, big_at[-4]))
+        gather_core_last(j, c, big_at[-4]).start()
     forward_own(7)
     for i in range(5, 8):
         from_sibling(i)
@@ -333,7 +325,9 @@
     offsets = [4, -3, 3, -1, 1, -2, 2, 0]
 
     def reduce_core(i, owner, place):
-        return remote(grads.at[owner, place], from_core.at[place], pair(sem_core, 1, i), sibling)
+        return remote(
+            grads.at[owner, place], from_core.at[place], (sem_send.at[3], sem_core.at[1, i]), sibling
+        )
 
     def own(offset, j):
         chunk = big_at[offset]
@@ -341,19 +335,19 @@
             (chunk, *at(j))
         ].astype(jnp.float32)
 
-    far_down = big(1, 0, out_far, in_far, down_two, FAR_DOWN)
-    far_up = big(1, 0, out_far, in_far, up_two, FAR_UP)
+    far_down = big(4, 16, out_far, in_far, down_two, FAR_DOWN)
+    far_up = big(4, 16, out_far, in_far, up_two, FAR_UP)
     three = [
-        big(1, 1, out_three.at[0], in_three.at[0], down),
-        big(1, 2, out_three.at[1], in_three.at[1], up),
+        big(4, 20, out_three.at[0], in_three.at[0], down),
+        big(4, 24, out_three.at[1], in_three.at[1], up),
+    ]
+    two = [
+        big(4, 28, out_two.at[0], in_two.at[0], down_two),
+        big(4, 32, out_two.at[1], in_two.at[1], up_two),
     ]
     one = [
-        big(1, 3, out_one.at[0], in_one.at[0], down),
-        big(1, 4, out_one.at[1], in_one.at[1], up),
-    ]
-    two = [
-        big(1, 5, out_two.at[0], in_two.at[0], down_two),
-        big(1, 6, out_two.at[1], in_two.at[1], up_two),
+        big(4, 36, out_one.at[0], in_one.at[0], down, each=False),
+        big(4, 37, out_one.at[1], in_one.at[1], up, each=False),
     ]
     far = {**dict(zip(FAR_DOWN, far_down)), **dict(zip(FAR_UP, far_up))}
 
@@ -373,15 +367,15 @@
                 low = value.astype(jnp.bfloat16)
                 if offset == 4:
                     out_far[at(j)] = low
-                    go(far[j])
+                    far[j].start()
                 else:
                     box, copies = {3: (out_three, three), 2: (out_two, two), 1: (out_one, one)}[abs(offset)]
                     box[(side, *at(j))] = low
-                    go(copies[side][j])
+                    copies[side][j].start()
 
     for i, offset in enumerate(offsets):
         backward(1 - c, big_at, small_at[offset])
-        go(reduce_core(i, 1 - c, small_at[offset]))
+        reduce_core(i, 1 - c, small_at[offset]).start()
         backward(c, small_at, big_at[offset])
         if 2 <= i < 7:
             pass_on(offsets[i - 2])
@@ -392,25 +386,29 @@
         remote(
             mine.at[p],
             from_peers.at[MIRROR[p]],
-            (sem_peers.at[0, 1, p], sem_peers.at[1, 1, MIRROR[p]]),
+            (sem_send.at[5], sem_peers.at[SUBS]),
             peers[p],
         )
         for p in range(1, len(PLACES))
     ]
+    for side in range(2):
+        landed(in_one.at[side], sem_big.at[36 + side])
     for j in reversed(range(SUBS)):
         value = own(0, j)
-        for box, copies in ((in_one, one), (in_two, two)):
-            for side in range(2):
-                copies[side][j].wait_recv()
-                value = value + box[(side, *at(j))].astype(jnp.float32)
+        for side in range(2):
+            value = value + in_one[(side, *at(j))].astype(jnp.float32)
+        for side in range(2):
+            two[side][j].wait_recv()
+            value = value + in_two[(side, *at(j))].astype(jnp.float32)
         mine[at(j)] = value.astype(jnp.bfloat16)
         for p in reversed(range(max(4 * j, 1), 4 * j + 4)):
-            go(reduce_peers[p - 1])
+            reduce_peers[p - 1].start()
     for load in loads[4:]:
         load.wait()
     grad_sum = mine[0].astype(jnp.float32)
+    others = pl.ds(1, len(PLACES) - 1)
+    landed(from_peers.at[others], sem_peers.at[SUBS])
     for p in range(1, len(PLACES)):
-        remote(mine.at[p], from_peers.at[p], pair(sem_peers, 1, p), sibling).wait_recv()
         grad_sum = grad_sum + from_peers[p].astype(jnp.float32)
 
     grad_weight = gain_used * grad_sum * root_scale / token_count
@@ -428,11 +426,17 @@
                 device_id_type=MESH,
             )
         )
-        go(rep_copies[-1])
+        rep_copies[-1].start()
 
     gain_sum = to_row(jnp.sum(grad_sum * low_weight, axis=1, keepdims=True) * root_scale)
     new_gain_ref[...] = adam_step(gain[...], gain_sum / token_count, gain_first[...], gain_second[...])
 
+    sent(full_w.at[c, b, others], 0)
+    sent(full_w.at[c, pl.ds(0, 7)], 1)
+    sent(full_w.at[c], 2)
+    sent(from_core, 3)
+    sent(from_core.at[pl.ds(0, 7)], 4)
+    sent(mine.at[others], 5)
     for copy in rep_copies:
         copy.wait_recv()
     average = drifts[0]
@@ -441,7 +445,7 @@
     average_ref[...] = average / n_rep
     inner_ref[...] = inner_weight
 
-    for copy in started:
+    for copy in rep_copies:
         copy.wait_send()
 
 
@@ -481,9 +485,10 @@
         pltpu.VMEM((2 * n, rows, head), low),
         pltpu.VMEM((n_rep, rows, head), wide),
         dma((9,)),
-        dma((2, 2, 2 * n)),
-        dma((2, 2, 7, SUBS)),
-        dma((2, 2, n + SUBS)),
+        dma((6,)),
+        dma((SUBS + 1,)),
+        dma((38,)),
+        dma((2, n)),
         dma((2, max(n_rep - 1, 1))),
     ]
     inner_weight, new_gain, average = pl.pallas_call(

time: 66.9 us -> 65.3 us (0.976)
  Pallas kernels: 64.9 us -> 63.3 us
    pallas_call x1, Pallas kernels: 64.9 us -> 63.3 us  [per_device(): pl.pallas_call(functools.partial(kernel, n, n_rep), out_shape=(pltpu.VMEM...]
where the time goes in v5:
time: 65.3 us; the launch traced here: 65.1 us
  Pallas kernels  63.3 us (97%)
  between operations  0.66 us (1%)
    pallas_call x1, Pallas kernels, per_device(): pl.pallas_call(functools.partial(kernel, n, n_rep), out_shape=(pltpu.VMEM...  63.3 us

profile of v5, /device:TPU:16, one launch (start us, length us, event | category | flops | bytes accessed | tf_op | source)
XLA Modules:
  0.0 65.1 jit_solution(4040538273009581322)
XLA Ops:
  0.6 0.0 copy-start
  0.6 0.0 copy-start.1
  0.7 63.3 %shard_map.129 = (f32[32,128]{1,0:T(8,128)S(1)}, f32[1,32]{1,0:T(1,128)S(1)}, f32[32,128]{1,0:T(8,128)S(1)}) custom-call(bf16[1,192,8192]{2,1,0:T(8,128)(2,1)} %acts_hbm.1, bf16[1,192,128]{2,1,0:T(8,128)(2,1)} %targets_hbm.1, f32[1,32,128]{2,1,0:T(8,128)} %weight_hbm.1, f32[1,32,128]{2,1,0:T(8,128)} %first_hbm.1, f32[1,32,128]{2,1,0:T(8,128)} %second_hbm.1, ...), custom_call_target="tpu_custom_call" | custom-call | flops 805306368 | bytes 3145728 | tf_op jit(solution)/shard_map/pallas_call | solution.py:494
  64.0 0.5 copy.15
  64.5 0.0 copy-done
  64.5 0.0 copy-done.1
  64.5 0.6 multiply_bitcast_fusion
Async XLA Ops:
  0.6 63.8 %copy-start = (f32[32,128]{1,0:T(8,128)S(1)}, f32[32,128]{1,0:T(8,128)}, u32[]{:S(2)}) copy-start(f32[32,128]{1,0:T(8,128)} %base_hbm.1) | copy-start | bytes 49156
  0.6 63.8 %copy-start.1 = (f32[32,128]{1,0:T(8,128)S(1)}, f32[32,128]{1,0:T(8,128)}, u32[]{:S(2)}) copy-start(f32[32,128]{1,0:T(8,128)} %param.19) | copy-start | bytes 49156

commit v6 on v5

--- a/solution.py
+++ b/solution.py
@@ -373,12 +373,33 @@
                     box[(side, *at(j))] = low
                     copies[side][j].start()
 
-    for i, offset in enumerate(offsets):
-        backward(1 - c, big_at, small_at[offset])
-        reduce_core(i, 1 - c, small_at[offset]).start()
-        backward(c, small_at, big_at[offset])
-        if 2 <= i < 7:
-            pass_on(offsets[i - 2])
+    def produce(owner, *steps):
+        for i in steps:
+            offset = offsets[i]
+            x_at = {k: small_at[k] * (1 - c) + big_at[k] * c for k in small_at}
+            z_at = {k: big_at[k] * (1 - c) + small_at[k] * c for k in small_at}
+            if owner == 0:
+                backward(0, x_at, z_at[offset])
+            else:
+                backward(1, z_at, x_at[offset])
+
+            @pl.when(c == 1 - owner)
+            def _():
+                reduce_core(i, 1 - c, small_at[offset]).start()
+
+    produce(0, 0, 1, 2)
+    produce(1, 0, 1, 2)
+    pass_on(4)
+    pass_on(-3)
+    pass_on(3)
+    produce(0, 3, 4)
+    produce(1, 3, 4)
+    pass_on(-1)
+    produce(0, 5, 6)
+    produce(1, 5, 6)
+    pass_on(1)
+    produce(0, 7)
+    produce(1, 7)
     pass_on(-2, 2)
     reduce_core(len(offsets) - 1, c, b).wait_recv()
 

time: 65.3 us -> 65.7 us (level)
  no operation moved by 1% of the time
where the time goes in v6:
time: 65.7 us; the launch traced here: 65.4 us
  Pallas kernels  63.6 us (97%)
  between operations  0.66 us (1%)
    pallas_call x1, Pallas kernels, per_device(): pl.pallas_call(functools.partial(kernel, n, n_rep), out_shape=(pltpu.VMEM...  63.6 us

profile of v6, /device:TPU:16, one launch (start us, length us, event | category | flops | bytes accessed | tf_op | source)
XLA Modules:
  0.0 65.4 jit_solution(9829970748822430979)
XLA Ops:
  0.6 0.0 copy-start
  0.6 0.0 copy-start.1
  0.7 63.6 %shard_map.129 = (f32[32,128]{1,0:T(8,128)S(1)}, f32[1,32]{1,0:T(1,128)S(1)}, f32[32,128]{1,0:T(8,128)S(1)}) custom-call(bf16[1,192,8192]{2,1,0:T(8,128)(2,1)} %acts_hbm.1, bf16[1,192,128]{2,1,0:T(8,128)(2,1)} %targets_hbm.1, f32[1,32,128]{2,1,0:T(8,128)} %weight_hbm.1, f32[1,32,128]{2,1,0:T(8,128)} %first_hbm.1, f32[1,32,128]{2,1,0:T(8,128)} %second_hbm.1, ...), custom_call_target="tpu_custom_call" | custom-call | flops 805306368 | bytes 3145728 | tf_op jit(solution)/shard_map/pallas_call | solution.py:515
  64.3 0.5 copy.15
  64.8 0.0 copy-done
  64.8 0.0 copy-done.1
  64.8 0.6 multiply_bitcast_fusion
Async XLA Ops:
  0.6 64.2 %copy-start = (f32[32,128]{1,0:T(8,128)S(1)}, f32[32,128]{1,0:T(8,128)}, u32[]{:S(2)}) copy-start(f32[32,128]{1,0:T(8,128)} %base_hbm.1) | copy-start | bytes 49156
  0.6 64.1 %copy-start.1 = (f32[32,128]{1,0:T(8,128)S(1)}, f32[32,128]{1,0:T(8,128)}, u32[]{:S(2)}) copy-start(f32[32,128]{1,0:T(8,128)} %param.19) | copy-start | bytes 49156
